TPU v7x, 128 devices: a whole 4x4x4 slice. The times are simulated.
128 devices in a mesh: lon: 8 (over x, z_lo), lat: 16 (over y, z_hi, core).
Axes of the slice: x: 4, y: 4, z: 4 (z_hi: 2, z_lo: 2; z = z_hi * 2 + z_lo), core: 2. Of those that a mesh axis runs over, the one named last changes fastest.
Arguments:
- prior_state: float32 [64, 64, 64, 256], P('lon', 'lat'), may hold values from -3 to 3
- courant: float32 [64, 64], P('lon', 'lat'), may hold values from 0.2 to 0.8
- cell_survival_rate: float32 [64], replicated, may hold values from 0.8 to 1
- geometry: float32 [16, 64, 128], replicated, may hold values from 0.005 to 0.05
- entry_tile: int32 [8, 16, 64], P('lon', 'lat'), may hold values from 0 to 31, as said below
- entry_column: int32 [8, 16, 64], P('lon', 'lat'), may hold values from 0 to 31
- entry_segment: int32 [8, 16, 64], P('lon', 'lat'), may hold values from 0 to 15
- entry_counts: int32 [8, 16], P('lon', 'lat'), may hold values from 1 to 64, as said below
- observed: float32 [4, 8, 32, 128], P(None, 'lon', 'lat'), may hold values from -6 to 6
- obs_weight: float32 [4, 8, 32, 128], P(None, 'lon', 'lat'), may hold values from 0.02 to 0.08
Outputs:
- start_state: float32 [64, 64, 64, 256], P('lon', 'lat')
- end_state: float32 [64, 64, 64, 256], P('lon', 'lat')
Inputs may be any that keep to these rules, and one draw needn't show every extreme that they name: The owning band entry_tile // 2 of every entry is the device's own latitude band or one beside it. Entries at positions at or beyond the device's count are padding and are ignored. `entry_counts`: some device holds exactly 64 live entries.
All inputs are finite; a program needn't handle non-finite values.
Results may differ from a plain program's by a relative error of at most 0.0003.
Values sent between devices are 32-bit elements; how exact they have to be, the bound alone decides.
A program may use at most 128 MiB of HBM per device.

v0:
```python
import jax
import jax.numpy as jnp
from jax import lax
from jax.sharding import PartitionSpec as P

STEPS = 4


diffusion = 0.08
highest = lax.Precision.HIGHEST


def from_behind(x, axis, by):
    devices = lax.axis_size(axis)
    return lax.ppermute(x, axis, [(i, (i + by) % devices) for i in range(devices)])


def extended(cells, sides, width):
    for axis, dim in sides:
        count = lax.axis_size(axis)
        ends = count - 1
        head = lax.slice_in_dim(cells, 0, width, axis=dim)
        tail = lax.slice_in_dim(cells, cells.shape[dim] - width, cells.shape[dim], axis=dim)
        cells = jnp.concatenate(
            [
                lax.ppermute(tail, axis, [(i, (i + 1) % count) for i in range(ends)]),
                cells,
                lax.ppermute(head, axis, [((i + 1) % count, i) for i in range(ends)]),
            ],
            axis=dim,
        )
    return cells


def predicted_state(current_state, courant_number_grid, decay_grid):
    upwind_plane = from_behind(current_state[-1:], "lon", 1)
    behind = jnp.concatenate([upwind_plane, current_state[:-1]], axis=0)
    padded = extended(current_state, (("lat", 1),), 1)
    spread = padded[:, 2:] + padded[:, :-2] - 2.0 * current_state
    moved = current_state - courant_number_grid * (current_state - behind) + diffusion * spread
    return decay_grid * moved


def state_mapping(gram_total):
    width_all = gram_total.shape[0]
    identity = jnp.eye(width_all - 1, dtype=jnp.float32)
    chol_lower = jnp.linalg.cholesky(identity + gram_total[1:, 1:])
    inverse = lax.linalg.triangular_solve(chol_lower, identity, left_side=True, lower=True)
    inner = jnp.dot(inverse, gram_total[1:, 0], precision=highest)
    weights = jnp.dot(inner, inverse, precision=highest)
    first_row = (jnp.arange(width_all) == 0).astype(jnp.float32)[None, :]
    lower_rows = jnp.concatenate([weights[:, None], inverse.T], axis=1)
    return jnp.concatenate([first_row, lower_rows], axis=0)


def shards(
    prior_state,
    courant,
    cell_survival_rate,
    geometry,
    entry_tile,
    entry_column,
    entry_segment,
    entry_counts,
    observed,
    obs_weight,
):
    lon_cells, lat_cells, alt_cells, width_all = prior_state.shape
    tile_dev = observed.shape[2]
    ray_count = observed.shape[3]
    tiles_here = entry_tile[0, 0]
    columns_here = entry_column[0, 0]
    slot_total = tiles_here.shape[0]
    slot_index = jnp.arange(slot_total, dtype=jnp.int32)
    live_slot = slot_index < entry_counts[0, 0]
    paths = geometry[entry_segment[0, 0]]
    courant_number_grid = courant[:, :, None, None]
    decay_grid = cell_survival_rate[None, None, :, None]
    my_band = lax.axis_index("lat")
    near_ids = (my_band - 1) * tile_dev + jnp.arange(3 * tile_dev, dtype=jnp.int32)
    near_select = ((tiles_here[None, :] == near_ids[:, None]) & live_slot[None, :]).astype(
        jnp.float32
    )
    current_state = prior_state
    lagged = prior_state
    for step_index in range(STEPS):
        current_state = predicted_state(current_state, courant_number_grid, decay_grid)
        columns = current_state.reshape(lon_cells * lat_cells, alt_cells, width_all)[columns_here]
        block_list = jnp.einsum("ear,eak->erk", paths, columns, precision=highest).reshape(
            slot_total, ray_count * width_all
        )
        near_sums = jnp.dot(near_select, block_list, precision=highest).reshape(
            3, tile_dev * ray_count, width_all
        )
        padded = extended(near_sums, (("lat", 0),), 1)
        own_sums = padded[0] + padded[2] + padded[4]
        projected = own_sums.reshape(tile_dev, ray_count, width_all)
        weight_now = obs_weight[step_index, 0]
        innovation = (observed[step_index, 0] - projected[:, :, 0]) * weight_now
        scaled = projected[:, :, 1:] * weight_now[:, :, None]
        mixed_rows = jnp.concatenate([innovation[:, :, None], scaled], axis=2).reshape(
            -1, width_all
        )
        gram_local = lax.dot_general(
            mixed_rows, mixed_rows, (((0,), (0,)), ((), ())), precision=highest
        )
        gram_total = lax.psum(gram_local, ("lon", "lat"))
        update = state_mapping(gram_total)
        current_state = jnp.dot(
            current_state.reshape(-1, width_all), update, precision=highest
        ).reshape(current_state.shape)
        lagged = jnp.dot(lagged.reshape(-1, width_all), update, precision=highest).reshape(
            lagged.shape
        )
    return (lagged, current_state)


def solution(mesh):
    placed = (
        P("lon", "lat", None, None),
        P("lon", "lat"),
        P(),
        P(),
        P("lon", "lat", None),
        P("lon", "lat", None),
        P("lon", "lat", None),
        P("lon", "lat"),
        P(None, "lon", "lat", None),
        P(None, "lon", "lat", None),
    )
    return jax.shard_map(
        shards,
        mesh=mesh,
        in_specs=placed,
        out_specs=(P("lon", "lat", None, None), P("lon", "lat", None, None)),
        check_vma=False,
    )
```

profile of v0, /device:TPU:1, one launch (start us, length us, event | category | flops | bytes accessed | tf_op | source)
XLA Modules:
  0.0 1130.5 jit_solution(16806848649555162507)
XLA Ops:
  9.7 3.3 collective-permute-start.1
  13.0 5.5 collective-permute-start.2
  23.0 12.2 %collective-permute-done = f32[1,4,64,256]{3,2,1,0:T(8,128)S(1)} collective-permute-done((f32[1,4,64,256]{3,2,1,0:T(8,128)}, f32[1,4,64,256]{3,2,1,0:T(8,128)S(1)}, u32[]{:S(2)}, u32[]{:S(2)}) %collective-permute-start) | collective-permute-done | bytes 262176 | tf_op jit(solution)/shard_map/ppermute | solution.py:15
  35.2 5.9 fusion.19
  41.1 4.3 gather_fusion.1
  45.4 9.7 fusion.133
  55.1 4.7 copy.126
  65.6 5.1 collective-permute-start.3
  76.9 144.8 %all-reduce.7.cloned.1.call-done = f32[256,256]{0,1:T(8,128)} async-done(((f32[256,256]{0,1:T(8,128)}), f32[256,256]{0,1:T(8,128)}) %all-reduce.7.cloned.1.call-update) | async-done | bytes 262160 | tf_op jit(solution)/shard_map/psum | solution.py:107
  224.0 11.7 %cholesky.228 = f32[128,128]{1,0:T(8,128)S(1)} custom-call(f32[128,128]{1,0:T(8,128)S(1)} %cholesky.376), custom_call_target="Cholesky" | custom-call | tf_op jit(solution)/shard_map/jit(cholesky)/cholesky | solution.py:47
  235.8 9.8 custom-call.17
  246.1 11.6 %cholesky.248 = f32[127,127]{1,0:T(8,128)S(1)} custom-call(f32[127,127]{1,0:T(8,128)S(1)} %convolution_subtract_fusion.7), custom_call_target="Cholesky" | custom-call | tf_op jit(solution)/shard_map/jit(cholesky)/cholesky | solution.py:47
  260.5 19.9 %custom-call.18 = f32[2,128,128]{1,2,0:T(8,128)S(1)} custom-call(f32[2,128,128]{2,1,0:T(8,128)S(1)} %pad_maximum_fusion.32), custom_call_target="InvertDiagBlocksLowerTriangular" | custom-call | tf_op jit(solution)/shard_map/triangular_solve/custom-call.0 | solution.py:48
  287.7 4.1 collective-permute-start.7
  292.9 14.8 %collective-permute-done.5 = f32[1,4,64,256]{3,2,1,0:T(8,128)S(1)} collective-permute-done((f32[1,4,64,256]{3,2,1,0:T(8,128)S(1)}, f32[1,4,64,256]{3,2,1,0:T(8,128)S(1)}, u32[]{:S(2)}, u32[]{:S(2)}) %collective-permute-start.5) | collective-permute-done | bytes 262176 | tf_op jit(solution)/shard_map/ppermute | solution.py:15
  310.0 4.3 gather_fusion.2
  314.3 9.6 fusion.134
  323.9 4.7 copy.128
  338.6 5.1 collective-permute-start.8
  351.8 141.7 %all-reduce.9.cloned.1.call-done = f32[256,256]{0,1:T(8,128)} async-done(((f32[256,256]{0,1:T(8,128)}), f32[256,256]{0,1:T(8,128)}) %all-reduce.9.cloned.1.call-update) | async-done | bytes 262160 | tf_op jit(solution)/shard_map/psum | solution.py:107
  498.2 11.7 %cholesky.266 = f32[128,128]{1,0:T(8,128)S(1)} custom-call(f32[128,128]{1,0:T(8,128)S(1)} %cholesky.379), custom_call_target="Cholesky" | custom-call | tf_op jit(solution)/shard_map/jit(cholesky)/cholesky | solution.py:47
  510.0 9.8 custom-call.19
  522.0 11.6 %cholesky.286 = f32[127,127]{1,0:T(8,128)S(1)} custom-call(f32[127,127]{1,0:T(8,128)S(1)} %convolution_subtract_fusion.6), custom_call_target="Cholesky" | custom-call | tf_op jit(solution)/shard_map/jit(cholesky)/cholesky | solution.py:47
  537.0 19.9 %custom-call.20 = f32[2,128,128]{1,2,0:T(8,128)S(1)} custom-call(f32[2,128,128]{2,1,0:T(8,128)S(1)} %pad_maximum_fusion.33), custom_call_target="InvertDiagBlocksLowerTriangular" | custom-call | tf_op jit(solution)/shard_map/triangular_solve/custom-call.0 | solution.py:48
  565.3 4.1 collective-permute-start.12
  570.5 14.8 %collective-permute-done.10 = f32[1,4,64,256]{3,2,1,0:T(8,128)S(1)} collective-permute-done((f32[1,4,64,256]{3,2,1,0:T(8,128)S(1)}, f32[1,4,64,256]{3,2,1,0:T(8,128)S(1)}, u32[]{:S(2)}, u32[]{:S(2)}) %collective-permute-start.10) | collective-permute-done | bytes 262176 | tf_op jit(solution)/shard_map/ppermute | solution.py:15
  587.5 4.3 gather_fusion.3
  591.9 9.6 fusion.135
  601.5 4.7 copy.130
  619.5 5.1 collective-permute-start.13
  634.4 140.0 %all-reduce.11.cloned.1.call-done = f32[256,256]{0,1:T(8,128)} async-done(((f32[256,256]{0,1:T(8,128)}), f32[256,256]{0,1:T(8,128)}) %all-reduce.11.cloned.1.call-update) | async-done | bytes 262160 | tf_op jit(solution)/shard_map/psum | solution.py:107
  779.9 11.7 %cholesky.304 = f32[128,128]{1,0:T(8,128)S(1)} custom-call(f32[128,128]{1,0:T(8,128)S(1)} %cholesky.382), custom_call_target="Cholesky" | custom-call | tf_op jit(solution)/shard_map/jit(cholesky)/cholesky | solution.py:47
  792.3 9.8 custom-call.21
  804.9 11.6 %cholesky.324 = f32[127,127]{1,0:T(8,128)S(1)} custom-call(f32[127,127]{1,0:T(8,128)S(1)} %convolution_subtract_fusion.5), custom_call_target="Cholesky" | custom-call | tf_op jit(solution)/shard_map/jit(cholesky)/cholesky | solution.py:47
  821.4 19.9 %custom-call.22 = f32[2,128,128]{1,2,0:T(8,128)S(1)} custom-call(f32[2,128,128]{2,1,0:T(8,128)S(1)} %pad_maximum_fusion.34), custom_call_target="InvertDiagBlocksLowerTriangular" | custom-call | tf_op jit(solution)/shard_map/triangular_solve/custom-call.0 | solution.py:48
  849.8 4.1 collective-permute-start.17
  854.9 3.3 fusion.45
  858.3 11.6 %collective-permute-done.15 = f32[1,4,64,256]{3,2,1,0:T(8,128)S(1)} collective-permute-done((f32[1,4,64,256]{3,2,1,0:T(8,128)S(1)}, f32[1,4,64,256]{3,2,1,0:T(8,128)S(1)}, u32[]{:S(2)}, u32[]{:S(2)}) %collective-permute-start.15) | collective-permute-done | bytes 262176 | tf_op jit(solution)/shard_map/ppermute | solution.py:15
  872.1 4.5 gather_fusion.4
  876.6 9.6 fusion.136
  886.2 4.7 copy.132
  900.8 5.3 collective-permute-start.18
  906.2 4.9 fusion.47
  920.5 135.8 %all-reduce.13.cloned.1.call-done = f32[256,256]{0,1:T(8,128)} async-done(((f32[256,256]{0,1:T(8,128)}), f32[256,256]{0,1:T(8,128)}) %all-reduce.13.cloned.1.call-update) | async-done | bytes 262160 | tf_op jit(solution)/shard_map/psum | solution.py:107
  1058.6 11.7 %cholesky.342 = f32[128,128]{1,0:T(8,128)S(1)} custom-call(f32[128,128]{1,0:T(8,128)S(1)} %cholesky.385), custom_call_target="Cholesky" | custom-call | tf_op jit(solution)/shard_map/jit(cholesky)/cholesky | solution.py:47
  1070.4 10.0 custom-call.23
  1080.9 11.6 %cholesky.362 = f32[127,127]{1,0:T(8,128)S(1)} custom-call(f32[127,127]{1,0:T(8,128)S(1)} %convolution_subtract_fusion.4), custom_call_target="Cholesky" | custom-call | tf_op jit(solution)/shard_map/jit(cholesky)/cholesky | solution.py:47
  1095.3 19.7 %custom-call.24 = f32[2,128,128]{1,2,0:T(8,128)S(1)} custom-call(f32[2,128,128]{2,1,0:T(8,128)S(1)} %pad_maximum_fusion.35), custom_call_target="InvertDiagBlocksLowerTriangular" | custom-call | tf_op jit(solution)/shard_map/triangular_solve/custom-call.0 | solution.py:48
  (282 shorter events, 150.7 us)
Async XLA Ops:
  7.2 15.1 %copy-start = (f32[16,64,128]{2,1,0:T(8,128)S(1)}, f32[16,64,128]{2,1,0:T(8,128)}, u32[]{:S(2)}) copy-start(f32[16,64,128]{2,1,0:T(8,128)} %param.16) | copy-start | bytes 1572868
  7.2 11.4 %copy-start.6 = (f32[8,4,64,256]{3,2,1,0:T(8,128)S(1)}, f32[8,4,64,256]{3,2,1,0:T(8,128)}, u32[]{:S(2)}) copy-start(f32[8,4,64,256]{3,2,1,0:T(8,128)} %param.13) | copy-start | bytes 6291460
  7.2 12.8 %copy-start.32 = (s32[1,1,64]{2,1,0:T(1,128)S(1)}, s32[1,1,64]{2,1,0:T(1,128)}, u32[]{:S(2)}) copy-start(s32[1,1,64]{2,1,0:T(1,128)} %param.19) | copy-start | bytes 772
  7.2 12.8 %copy-start.33 = (s32[1,1,64]{2,1,0:T(1,128)S(1)}, s32[1,1,64]{2,1,0:T(1,128)}, u32[]{:S(2)}) copy-start(s32[1,1,64]{2,1,0:T(1,128)} %param.18) | copy-start | bytes 772
  7.2 214.5 %all-reduce.7.cloned.1.call-start = ((), (), s32[]{:S(2)}) async-start(), calls=%async_computation | async-start | bytes 524288 | tf_op jit(solution)/shard_map/psum | solution.py:107
  9.7 25.5 %collective-permute-start.1 = (f32[8,1,64,256]{3,2,1,0:T(8,128)}, f32[8,1,64,256]{3,2,1,0:T(8,128)S(1)}, u32[]{:S(2)}, u32[]{:S(2)}) collective-permute-start(f32[8,1,64,256]{3,2,1,0:T(8,128)} %get-tuple-element.48), channel_id=1, source_target_pairs={{1,0},{2,1},{3,2},{4,3},{5,4},{6,5},{7,6},{8,7},{9,8},{10,9},{11,1... | collective-permute-start | bytes 1572872 | tf_op jit(solution)/shard_map/ppermute | solution.py:28
  13.0 8.5 copy-start.31
  13.0 22.1 %collective-permute-start.2 = (f32[8,1,64,256]{3,2,1,0:T(8,128)}, f32[8,1,64,256]{3,2,1,0:T(8,128)}, u32[]{:S(2)}, u32[]{:S(2)}) collective-permute-start(f32[8,1,64,256]{3,2,1,0:T(8,128)} %get-tuple-element.49), channel_id=1, source_target_pairs={{0,1},{1,2},{2,3},{3,4},{4,5},{5,6},{6,7},{7,8},{8,9},{9,10},{10,1... | collective-permute-start | bytes 1572872 | tf_op jit(solution)/shard_map/ppermute | solution.py:26
  19.3 15.9 %collective-permute-start = (f32[1,4,64,256]{3,2,1,0:T(8,128)}, f32[1,4,64,256]{3,2,1,0:T(8,128)S(1)}, u32[]{:S(2)}, u32[]{:S(2)}) collective-permute-start(f32[1,4,64,256]{3,2,1,0:T(8,128)} %slice.276), channel_id=1, source_target_pairs={{0,16},{16,32},{32,48},{48,64},{64,80},{80,96},{96,112},{112,0},{1... | collective-permute-start | bytes 786440 | tf_op jit(solution)/shard_map/ppermute | solution.py:15
  20.1 586.2 %copy-start.25 = (s32[6]{0:T(128)}, s32[6]{0:T(128)S(1)}, u32[]{:S(2)}) copy-start(s32[6]{0:T(128)S(1)} %iota_add_fusion) | copy-start | bytes 76
  22.2 12.9 %copy-start.21 = (f32[64]{0:T(128)S(1)}, f32[64]{0:T(128)}, u32[]{:S(2)}) copy-start(f32[64]{0:T(128)} %param.15) | copy-start | bytes 772
  23.0 583.3 %copy-start.27 = (pred[64]{0:T(512)(128)(4,1)}, pred[64]{0:T(512)(128)(4,1)S(1)}, u32[]{:S(2)}) copy-start(pred[64]{0:T(512)(128)(4,1)S(1)} %iota_compare_fusion.7) | copy-start | bytes 196
  23.0 564.5 %copy-start.20 = (s32[1024]{0:T(1024)}, s32[1024]{0:T(1024)S(1)}, u32[]{:S(2)}) copy-start(s32[1024]{0:T(1024)S(1)} %pad_clamp_fusion) | copy-start | bytes 12292
  62.6 8.1 copy-start.17
  63.3 9.2 collective-permute-start.4
  65.5 9.8 copy-start.30
  65.6 8.4 collective-permute-start.3
  76.6 183.8 %copy-start.11 = (f32[128,1]{1,0:T(8,128)S(1)}, f32[128,1]{1,0:T(8,128)}, u32[]{:S(2)}) copy-start(f32[128,1]{1,0:T(8,128)} %constant.77.clone.4) | copy-start | bytes 1540
  76.6 416.9 %all-reduce.9.cloned.1.call-start = ((), (), s32[]{:S(2)}) async-start(), calls=%async_computation.1 | async-start | bytes 524288 | tf_op jit(solution)/shard_map/psum | solution.py:107
  284.8 23.0 %collective-permute-start.6 = (f32[8,1,64,256]{3,2,1,0:T(8,128)S(1)}, f32[8,1,64,256]{3,2,1,0:T(8,128)S(1)}, u32[]{:S(2)}, u32[]{:S(2)}) collective-permute-start(f32[8,1,64,256]{3,2,1,0:T(8,128)S(1)} %get-tuple-element.46), channel_id=1, source_target_pairs={{1,0},{2,1},{3,2},{4,3},{5,4},{6,5},{7,6},{8,7},{9,8},{10,9},{11,1... | collective-permute-start | bytes 1572872 | tf_op jit(solution)/shard_map/ppermute | solution.py:28
  287.7 20.1 %collective-permute-start.7 = (f32[8,1,64,256]{3,2,1,0:T(8,128)S(1)}, f32[8,1,64,256]{3,2,1,0:T(8,128)S(1)}, u32[]{:S(2)}, u32[]{:S(2)}) collective-permute-start(f32[8,1,64,256]{3,2,1,0:T(8,128)S(1)} %get-tuple-element.47), channel_id=1, source_target_pairs={{0,1},{1,2},{2,3},{3,4},{4,5},{5,6},{6,7},{7,8},{8,9},{9,10},{10,1... | collective-permute-start | bytes 1572872 | tf_op jit(solution)/shard_map/ppermute | solution.py:26
  291.9 15.9 %collective-permute-start.5 = (f32[1,4,64,256]{3,2,1,0:T(8,128)S(1)}, f32[1,4,64,256]{3,2,1,0:T(8,128)S(1)}, u32[]{:S(2)}, u32[]{:S(2)}) collective-permute-start(f32[1,4,64,256]{3,2,1,0:T(8,128)S(1)} %bitcast.335), channel_id=1, source_target_pairs={{0,16},{16,32},{32,48},{48,64},{64,80},{80,96},{96,112},{112,0},{1... | collective-permute-start | bytes 786440 | tf_op jit(solution)/shard_map/ppermute | solution.py:15
  334.6 10.9 collective-permute-start.9
  338.6 8.8 collective-permute-start.8
  351.6 422.9 %all-reduce.11.cloned.1.call-start = ((), (), s32[]{:S(2)}) async-start(), calls=%async_computation.2 | async-start | bytes 524288 | tf_op jit(solution)/shard_map/psum | solution.py:107
  562.3 23.0 %collective-permute-start.11 = (f32[8,1,64,256]{3,2,1,0:T(8,128)S(1)}, f32[8,1,64,256]{3,2,1,0:T(8,128)S(1)}, u32[]{:S(2)}, u32[]{:S(2)}) collective-permute-start(f32[8,1,64,256]{3,2,1,0:T(8,128)S(1)} %get-tuple-element.44), channel_id=1, source_target_pairs={{1,0},{2,1},{3,2},{4,3},{5,4},{6,5},{7,6},{8,7},{9,8},{10,9},{11,1... | collective-permute-start | bytes 1572872 | tf_op jit(solution)/shard_map/ppermute | solution.py:28
  565.3 20.1 %collective-permute-start.12 = (f32[8,1,64,256]{3,2,1,0:T(8,128)S(1)}, f32[8,1,64,256]{3,2,1,0:T(8,128)S(1)}, u32[]{:S(2)}, u32[]{:S(2)}) collective-permute-start(f32[8,1,64,256]{3,2,1,0:T(8,128)S(1)} %get-tuple-element.45), channel_id=1, source_target_pairs={{0,1},{1,2},{2,3},{3,4},{4,5},{5,6},{6,7},{7,8},{8,9},{9,10},{10,1... | collective-permute-start | bytes 1572872 | tf_op jit(solution)/shard_map/ppermute | solution.py:26
  569.4 15.9 %collective-permute-start.10 = (f32[1,4,64,256]{3,2,1,0:T(8,128)S(1)}, f32[1,4,64,256]{3,2,1,0:T(8,128)S(1)}, u32[]{:S(2)}, u32[]{:S(2)}) collective-permute-start(f32[1,4,64,256]{3,2,1,0:T(8,128)S(1)} %bitcast.336), channel_id=1, source_target_pairs={{0,16},{16,32},{32,48},{48,64},{64,80},{80,96},{96,112},{112,0},{1... | collective-permute-start | bytes 786440 | tf_op jit(solution)/shard_map/ppermute | solution.py:15
  613.9 14.2 %collective-permute-start.14 = (f32[1,256,256]{1,2,0:T(8,128)}, f32[1,256,256]{1,2,0:T(8,128)}, u32[]{:S(2)}, u32[]{:S(2)}) collective-permute-start(f32[1,256,256]{1,2,0:T(8,128)} %copy.97), channel_id=1, source_target_pairs={{1,0},{2,1},{3,2},{4,3},{5,4},{6,5},{7,6},{8,7},{9,8},{10,9},{11,1... | collective-permute-start | bytes 786440 | tf_op jit(solution)/shard_map/ppermute | solution.py:28
  619.5 10.4 collective-permute-start.13
  634.2 422.1 %all-reduce.13.cloned.1.call-start = ((), (), s32[]{:S(2)}) async-start(), calls=%async_computation.3 | async-start | bytes 524288 | tf_op jit(solution)/shard_map/psum | solution.py:107
  846.7 8.3 copy-start.7
  846.7 23.2 %collective-permute-start.16 = (f32[8,1,64,256]{3,2,1,0:T(8,128)S(1)}, f32[8,1,64,256]{3,2,1,0:T(8,128)S(1)}, u32[]{:S(2)}, u32[]{:S(2)}) collective-permute-start(f32[8,1,64,256]{3,2,1,0:T(8,128)S(1)} %get-tuple-element.42), channel_id=1, source_target_pairs={{1,0},{2,1},{3,2},{4,3},{5,4},{6,5},{7,6},{8,7},{9,8},{10,9},{11,1... | collective-permute-start | bytes 1572872 | tf_op jit(solution)/shard_map/ppermute | solution.py:28
  849.8 20.1 %collective-permute-start.17 = (f32[8,1,64,256]{3,2,1,0:T(8,128)S(1)}, f32[8,1,64,256]{3,2,1,0:T(8,128)S(1)}, u32[]{:S(2)}, u32[]{:S(2)}) collective-permute-start(f32[8,1,64,256]{3,2,1,0:T(8,128)S(1)} %get-tuple-element.43), channel_id=1, source_target_pairs={{0,1},{1,2},{2,3},{3,4},{4,5},{5,6},{6,7},{7,8},{8,9},{9,10},{10,1... | collective-permute-start | bytes 1572872 | tf_op jit(solution)/shard_map/ppermute | solution.py:26
  854.0 15.9 %collective-permute-start.15 = (f32[1,4,64,256]{3,2,1,0:T(8,128)S(1)}, f32[1,4,64,256]{3,2,1,0:T(8,128)S(1)}, u32[]{:S(2)}, u32[]{:S(2)}) collective-permute-start(f32[1,4,64,256]{3,2,1,0:T(8,128)S(1)} %bitcast.334), channel_id=1, source_target_pairs={{0,16},{16,32},{32,48},{48,64},{64,80},{80,96},{96,112},{112,0},{1... | collective-permute-start | bytes 786440 | tf_op jit(solution)/shard_map/ppermute | solution.py:15
  858.2 11.7 %copy-start.22 = (f32[64]{0:T(128)S(1)}, f32[64]{0:T(128)}, u32[]{:S(2)}) copy-start(f32[64]{0:T(128)} %param.15) | copy-start | bytes 772
  886.2 4.8 copy-start.24
  886.2 4.8 copy-start.26
  886.2 4.8 copy-start.28
  893.8 12.3 %copy-start.9 = (f32[256,2048]{1,0:T(8,128)S(1)}, f32[256,2048]{1,0:T(8,128)}, u32[]{:S(2)}) copy-start(f32[256,2048]{1,0:T(8,128)} %fusion.45) | copy-start | bytes 6291460
  896.9 14.3 %collective-permute-start.19 = (f32[1,256,256]{1,2,0:T(8,128)}, f32[1,256,256]{1,2,0:T(8,128)}, u32[]{:S(2)}, u32[]{:S(2)}) collective-permute-start(f32[1,256,256]{1,2,0:T(8,128)} %copy.105), channel_id=1, source_target_pairs={{1,0},{2,1},{3,2},{4,3},{5,4},{6,5},{7,6},{8,7},{9,8},{10,9},{11,1... | collective-permute-start | bytes 786440 | tf_op jit(solution)/shard_map/ppermute | solution.py:28
  900.8 11.6 %collective-permute-start.18 = (f32[1,256,256]{1,2,0:T(8,128)}, f32[1,256,256]{1,2,0:T(8,128)}, u32[]{:S(2)}, u32[]{:S(2)}) collective-permute-start(f32[1,256,256]{1,2,0:T(8,128)} %copy.103), channel_id=1, source_target_pairs={{0,1},{1,2},{2,3},{3,4},{4,5},{5,6},{6,7},{7,8},{8,9},{9,10},{10,1... | collective-permute-start | bytes 786440 | tf_op jit(solution)/shard_map/ppermute | solution.py:26
  911.0 4.9 copy-start.29
  911.2 6.1 copy-start.10
  911.2 6.1 copy-start.19
  920.5 174.6 %copy-start.12 = (f32[128,1]{1,0:T(8,128)S(1)}, f32[128,1]{1,0:T(8,128)}, u32[]{:S(2)}) copy-start(f32[128,1]{1,0:T(8,128)} %constant.77.clone.4) | copy-start | bytes 1540
  1070.4 46.9 %copy-start.2 = (f32[8,4,64,256]{3,2,1,0:T(8,128)S(1)}, f32[8,4,64,256]{3,2,1,0:T(8,128)}, u32[]{:S(2)}) copy-start(f32[8,4,64,256]{3,2,1,0:T(8,128)} %fusion.4) | copy-start | bytes 6291460
  1117.3 6.5 copy-start.1
  (10 other events, 21.8 us)
Sparse Core Ops, SparseCore 0:
  76.7 144.9 all-reduce.6
  351.7 141.7 all-reduce.8
  634.3 140.0 all-reduce.10
  917.4 138.8 all-reduce.12
where the time goes:
time: 1140 us; the launch traced here: 1130 us
  waiting for transfers between devices  619 us (54%)
  other arithmetic  247 us (22%)
  matrix products  94.8 us (8%)
  local copies, waits for them, and re-layouts  85.8 us (8%)
  starting transfers between devices  62.8 us (6%)
  between operations  21.1 us (2%)
    psum x4, waiting for transfers between devices, shards(): gram_total = lax.psum(gram_local, ('lon', 'lat'))  562 us
    another operation x28, other arithmetic, state_mapping(): chol_lower = jnp.linalg.cholesky(identity + gram_total[1:, 1:])  139 us
    another operation x16, other arithmetic, state_mapping(): lax.linalg.triangular_solve(chol_lower, identity, left_side=True, lower=T...  80.8 us
    ppermute x4, waiting for transfers between devices, from_behind(): lax.ppermute(x, axis, [(i, (i + by) % devices) for i in range(devices)])  53.4 us
    ppermute x8, starting transfers between devices, extended(): lax.ppermute(tail, axis, [(i, (i + 1) % count) for i in range(ends)])  38.6 us
    dot_general x4, matrix products, shards(): jnp.einsum('ear,eak->erk', paths, columns, precision=highest)  38.5 us
    unnamed x77, local copies, waits for them, and re-layouts  24.6 us
  transfers between devices with their start and end apart: 24, of which 11 were waited for; matrix products, arithmetic and copies ran while one was open for 3% of the time, Pallas kernels for 0%

commit v1 on v0

--- a/solution.py
+++ b/solution.py
@@ -82,7 +82,7 @@
         jnp.float32
     )
     current_state = prior_state
-    lagged = prior_state
+    gram_local = jnp.zeros((width_all, width_all), jnp.float32)
     for step_index in range(STEPS):
         current_state = predicted_state(current_state, courant_number_grid, decay_grid)
         columns = current_state.reshape(lon_cells * lat_cells, alt_cells, width_all)[columns_here]
@@ -101,18 +101,18 @@
         mixed_rows = jnp.concatenate([innovation[:, :, None], scaled], axis=2).reshape(
             -1, width_all
         )
-        gram_local = lax.dot_general(
+        gram_local = gram_local + lax.dot_general(
             mixed_rows, mixed_rows, (((0,), (0,)), ((), ())), precision=highest
         )
-        gram_total = lax.psum(gram_local, ("lon", "lat"))
-        update = state_mapping(gram_total)
-        current_state = jnp.dot(
-            current_state.reshape(-1, width_all), update, precision=highest
-        ).reshape(current_state.shape)
-        lagged = jnp.dot(lagged.reshape(-1, width_all), update, precision=highest).reshape(
-            lagged.shape
-        )
-    return (lagged, current_state)
+    gram_total = lax.psum(gram_local, ("lon", "lat"))
+    update = state_mapping(gram_total)
+    end_state = jnp.dot(
+        current_state.reshape(-1, width_all), update, precision=highest
+    ).reshape(current_state.shape)
+    start_state = jnp.dot(
+        prior_state.reshape(-1, width_all), update, precision=highest
+    ).reshape(prior_state.shape)
+    return (start_state, end_state)
 
 
 def solution(mesh):

time: 1140 us -> 461 us (0.40)
  waiting for transfers between devices: 619 us -> 170 us
  other arithmetic: 247 us -> 74.7 us
  matrix products: 94.8 us -> 60.1 us
  local copies, waits for them, and re-layouts: 85.8 us -> 68.2 us
    psum x4 -> x1, waiting for transfers between devices: 562 us -> 149 us  [shards(): gram_total = lax.psum(gram_local, ('lon', 'lat'))]
    another operation x28 -> x7, other arithmetic: 139 us -> 34.7 us  [state_mapping(): chol_lower = jnp.linalg.cholesky(identity + gram_total[1:, 1:])]
    another operation x16 -> x4, other arithmetic: 80.8 us -> 19.8 us  [state_mapping(): lax.linalg.triangular_solve(chol_lower, identity, left_side=True, lower=T...]
    ppermute x4, waiting for transfers between devices: 53.4 us -> 20.7 us  [from_behind(): lax.ppermute(x, axis, [(i, (i + by) % devices) for i in range(devices)])]
    dot_general x4 -> x1, matrix products: 14.6 us -> 1.94 us  [shards(): jnp.dot(prior_state.reshape(-1, width_all), update, precision=highest)]
    unnamed x77 -> x69, local copies, waits for them, and re-layouts: 24.6 us -> 19.7 us
  transfers between devices with their start and end apart: 24 -> 21, of which waited for: 11 -> 5; matrix products, arithmetic and copies ran while one was open for 3% -> 21% of each run, Pallas kernels for 0% -> 0%
where the time goes in v1:
time: 461 us; the launch traced here: 454 us
  waiting for transfers between devices  170 us (37%)
  other arithmetic  74.7 us (16%)
  local copies, waits for them, and re-layouts  68.2 us (15%)
  starting transfers between devices  63.8 us (14%)
  matrix products  60.1 us (13%)
  between operations  17.3 us (4%)
    psum x1, waiting for transfers between devices, shards(): gram_total = lax.psum(gram_local, ('lon', 'lat'))  149 us
    ppermute x8, starting transfers between devices, extended(): lax.ppermute(tail, axis, [(i, (i + 1) % count) for i in range(ends)])  41.7 us
    dot_general x4, matrix products, shards(): jnp.einsum('ear,eak->erk', paths, columns, precision=highest)  38.7 us
    another operation x7, other arithmetic, state_mapping(): chol_lower = jnp.linalg.cholesky(identity + gram_total[1:, 1:])  34.7 us
    ppermute x4, waiting for transfers between devices, from_behind(): lax.ppermute(x, axis, [(i, (i + by) % devices) for i in range(devices)])  20.7 us
    another operation x4, other arithmetic, state_mapping(): lax.linalg.triangular_solve(chol_lower, identity, left_side=True, lower=T...  19.8 us
    unnamed x69, local copies, waits for them, and re-layouts  19.7 us
    ppermute x8, starting transfers between devices, extended(): lax.ppermute(head, axis, [((i + 1) % count, i) for i in range(ends)])  16.7 us
  transfers between devices with their start and end apart: 21, of which 5 were waited for; matrix products, arithmetic and copies ran while one was open for 21% of the time, Pallas kernels for 0%

profile of v1, /device:TPU:1, one launch (start us, length us, event | category | flops | bytes accessed | tf_op | source)
XLA Modules:
  0.0 454.5 jit_solution(9031396671559683551)
XLA Ops:
  7.3 2.5 fusion.79
  9.7 3.3 collective-permute-start.1
  13.0 5.5 %collective-permute-start.2 = (f32[8,1,64,256]{3,2,1,0:T(8,128)}, f32[8,1,64,256]{3,2,1,0:T(8,128)}, u32[]{:S(2)}, u32[]{:S(2)}) collective-permute-start(f32[8,1,64,256]{3,2,1,0:T(8,128)} %get-tuple-element.31), channel_id=1, source_target_pairs={{0,1},{1,2},{2,3},{3,4},{4,5},{5,6},{6,7},{7,8},{8,9},{9,10},{10,1... | collective-permute-start | bytes 1572872 | tf_op jit(solution)/shard_map/ppermute | solution.py:26
  22.2 2.0 gather_fusion
  24.8 10.4 %collective-permute-done = f32[1,4,64,256]{3,2,1,0:T(8,128)S(1)} collective-permute-done((f32[1,4,64,256]{3,2,1,0:T(8,128)}, f32[1,4,64,256]{3,2,1,0:T(8,128)S(1)}, u32[]{:S(2)}, u32[]{:S(2)}) %collective-permute-start) | collective-permute-done | bytes 262176 | tf_op jit(solution)/shard_map/ppermute | solution.py:15
  35.2 4.4 fusion.19
  43.4 5.1 %collective-permute-start.7 = (f32[8,1,64,256]{3,2,1,0:T(8,128)}, f32[8,1,64,256]{3,2,1,0:T(8,128)}, u32[]{:S(2)}, u32[]{:S(2)}) collective-permute-start(f32[8,1,64,256]{3,2,1,0:T(8,128)} %get-tuple-element.29), channel_id=1, source_target_pairs={{0,1},{1,2},{2,3},{3,4},{4,5},{5,6},{6,7},{7,8},{8,9},{9,10},{10,1... | collective-permute-start | bytes 1572872 | tf_op jit(solution)/shard_map/ppermute | solution.py:26
  50.4 2.8 gather_fusion.1
  53.2 9.7 %fusion.84 = f32[64,128,256]{2,1,0:T(8,128)S(1)} fusion(f32[64,64,128]{2,1,0:T(8,128)} %gather_fusion, f32[64,64,256]{2,1,0:T(8,128)} %gather_fusion.1), kind=kOutput, calls=%fused_computation.165 | convolution fusion | flops 1610612736 | bytes 14680064 | tf_op jit(solution)/shard_map/ear,eak->erk/dot_general | solution.py:89
  63.0 4.7 %copy.109 = f32[8,8,128,256]{3,1,2,0:T(8,128)S(1)} copy(f32[8,8,128,256]{3,2,1,0:T(8,128)S(1)} %bitcast.170) | data formatting | bytes 16777216
  67.7 2.8 fusion.52
  73.3 1.9 collective-permute-start.4
  76.3 5.1 %collective-permute-start.3 = (f32[1,256,256]{1,2,0:T(8,128)}, f32[1,256,256]{1,2,0:T(8,128)}, u32[]{:S(2)}, u32[]{:S(2)}) collective-permute-start(f32[1,256,256]{1,2,0:T(8,128)} %copy.70), channel_id=1, source_target_pairs={{0,1},{1,2},{2,3},{3,4},{4,5},{5,6},{6,7},{7,8},{8,9},{9,10},{10,1... | collective-permute-start | bytes 786440 | tf_op jit(solution)/shard_map/ppermute | solution.py:26
  81.5 4.6 %fusion.14 = f32[8,4,64,256]{3,2,1,0:T(8,128)S(1)} fusion(f32[8,4,64,256]{3,2,1,0:T(8,128)} %copy-done.4, f32[8,1,64,256]{3,2,1,0:T(8,128)} %collective-permute-done.7, f32[8,1,64,256]{3,2,1,0:T(8,128)} %collective-permute-done.6, f32[7,4,64,256]{3,2,1,0:T(8,128)} %slice.337, f32[1,4,64,256]{3,2,1,0:T(8,128)S(1)} %collective-permute-done.5, ...), kind=kLoop, calls=%fused_computation.25 | loop fusion | flops 6291456 | bytes 7340416 | tf_op jit(solution)/shard_map/mul | solution.py:41
  86.1 2.8 gather_fusion.2
  88.9 9.9 %fusion.85 = f32[64,128,256]{2,1,0:T(8,128)S(1)} fusion(f32[64,64,128]{2,1,0:T(8,128)} %gather_fusion, f32[64,64,256]{2,1,0:T(8,128)} %gather_fusion.2), kind=kOutput, calls=%fused_computation.166 | convolution fusion | flops 1610612736 | bytes 14680064 | tf_op jit(solution)/shard_map/ear,eak->erk/dot_general | solution.py:89
  98.8 4.7 %copy.111 = f32[8,8,128,256]{3,1,2,0:T(8,128)S(1)} copy(f32[8,8,128,256]{3,2,1,0:T(8,128)S(1)} %bitcast.171) | data formatting | bytes 16777216
  103.6 2.8 fusion.51
  107.8 1.9 collective-permute-start.9
  110.7 5.1 %collective-permute-start.8 = (f32[1,256,256]{1,2,0:T(8,128)}, f32[1,256,256]{1,2,0:T(8,128)}, u32[]{:S(2)}, u32[]{:S(2)}) collective-permute-start(f32[1,256,256]{1,2,0:T(8,128)} %copy.75), channel_id=1, source_target_pairs={{0,1},{1,2},{2,3},{3,4},{4,5},{5,6},{6,7},{7,8},{8,9},{9,10},{10,1... | collective-permute-start | bytes 786440 | tf_op jit(solution)/shard_map/ppermute | solution.py:26
  117.0 1.9 collective-permute-start.11
  118.9 5.1 %collective-permute-start.12 = (f32[8,1,64,256]{3,2,1,0:T(8,128)}, f32[8,1,64,256]{3,2,1,0:T(8,128)}, u32[]{:S(2)}, u32[]{:S(2)}) collective-permute-start(f32[8,1,64,256]{3,2,1,0:T(8,128)} %get-tuple-element.27), channel_id=1, source_target_pairs={{0,1},{1,2},{2,3},{3,4},{4,5},{5,6},{6,7},{7,8},{8,9},{9,10},{10,1... | collective-permute-start | bytes 1572872 | tf_op jit(solution)/shard_map/ppermute | solution.py:26
  132.3 7.9 %collective-permute-done.10 = f32[1,4,64,256]{3,2,1,0:T(8,128)} collective-permute-done((f32[1,4,64,256]{3,2,1,0:T(8,128)}, f32[1,4,64,256]{3,2,1,0:T(8,128)}, u32[]{:S(2)}, u32[]{:S(2)}) %collective-permute-start.10) | collective-permute-done | bytes 262176 | tf_op jit(solution)/shard_map/ppermute | solution.py:15
  140.2 2.7 fusion.9
  145.3 4.5 gather_fusion.3
  149.8 9.4 %fusion.86 = f32[64,128,256]{2,1,0:T(8,128)S(1)} fusion(f32[64,64,128]{2,1,0:T(8,128)S(1)} %copy-done.5, f32[64,64,256]{2,1,0:T(8,128)} %gather_fusion.3), kind=kOutput, calls=%fused_computation.167 | convolution fusion | flops 1610612736 | bytes 14680064 | tf_op jit(solution)/shard_map/ear,eak->erk/dot_general | solution.py:89
  159.2 4.7 %copy.113 = f32[8,8,128,256]{3,1,2,0:T(8,128)S(1)} copy(f32[8,8,128,256]{3,2,1,0:T(8,128)S(1)} %bitcast.172) | data formatting | bytes 16777216
  164.0 2.8 fusion.50
  166.8 1.9 collective-permute-start.16
  168.8 5.1 %collective-permute-start.17 = (f32[8,1,64,256]{3,2,1,0:T(8,128)}, f32[8,1,64,256]{3,2,1,0:T(8,128)}, u32[]{:S(2)}, u32[]{:S(2)}) collective-permute-start(f32[8,1,64,256]{3,2,1,0:T(8,128)} %get-tuple-element.25), channel_id=1, source_target_pairs={{0,1},{1,2},{2,3},{3,4},{4,5},{5,6},{6,7},{7,8},{8,9},{9,10},{10,1... | collective-permute-start | bytes 1572872 | tf_op jit(solution)/shard_map/ppermute | solution.py:26
  173.9 2.2 collective-permute-start.15
  178.2 1.9 collective-permute-start.14
  181.2 5.1 %collective-permute-start.13 = (f32[1,256,256]{1,2,0:T(8,128)}, f32[1,256,256]{1,2,0:T(8,128)}, u32[]{:S(2)}, u32[]{:S(2)}) collective-permute-start(f32[1,256,256]{1,2,0:T(8,128)} %copy.82), channel_id=1, source_target_pairs={{0,1},{1,2},{2,3},{3,4},{4,5},{5,6},{6,7},{7,8},{8,9},{9,10},{10,1... | collective-permute-start | bytes 786440 | tf_op jit(solution)/shard_map/ppermute | solution.py:26
  186.3 2.4 collective-permute-done.15
  188.8 4.0 fusion.4
  192.8 4.5 gather_fusion.4
  197.3 9.6 %fusion.87 = f32[64,128,256]{2,1,0:T(8,128)S(1)} fusion(f32[64,64,128]{2,1,0:T(8,128)S(1)} %copy-done.6, f32[64,64,256]{2,1,0:T(8,128)} %gather_fusion.4), kind=kOutput, calls=%fused_computation.168 | convolution fusion | flops 1610612736 | bytes 14680064 | tf_op jit(solution)/shard_map/ear,eak->erk/dot_general | solution.py:89
  206.9 4.7 %copy.115 = f32[8,8,128,256]{3,1,2,0:T(8,128)S(1)} copy(f32[8,8,128,256]{3,2,1,0:T(8,128)S(1)} %bitcast.169) | data formatting | bytes 16777216
  211.7 2.8 fusion.49
  215.2 1.9 collective-permute-start.19
  217.5 5.3 %collective-permute-start.18 = (f32[1,256,256]{1,2,0:T(8,128)S(1)}, f32[1,256,256]{1,2,0:T(8,128)S(1)}, u32[]{:S(2)}, u32[]{:S(2)}) collective-permute-start(f32[1,256,256]{1,2,0:T(8,128)S(1)} %copy.88), channel_id=1, source_target_pairs={{0,1},{1,2},{2,3},{3,4},{4,5},{5,6},{6,7},{7,8},{8,9},{9,10},{10,1... | collective-permute-start | bytes 786440 | tf_op jit(solution)/shard_map/ppermute | solution.py:26
  230.0 149.4 %all-reduce.4.cloned.1.call-done = f32[256,256]{0,1:T(8,128)} async-done(((f32[256,256]{0,1:T(8,128)}), f32[256,256]{0,1:T(8,128)}) %all-reduce.4.cloned.1.call-update) | async-done | bytes 262160 | tf_op jit(solution)/shard_map/psum | solution.py:107
  381.7 11.7 %cholesky.51 = f32[128,128]{1,0:T(8,128)S(1)} custom-call(f32[128,128]{1,0:T(8,128)S(1)} %cholesky.124), custom_call_target="Cholesky" | custom-call | tf_op jit(solution)/shard_map/jit(cholesky)/cholesky | solution.py:47
  393.5 9.8 %custom-call.14 = f32[1,128,128]{1,2,0:T(8,128)S(1)} custom-call(f32[1,128,128]{2,1,0:T(8,128)S(1)} %get-tuple-element.47), custom_call_target="InvertDiagBlocksLowerTriangular" | custom-call | tf_op jit(solution)/shard_map/jit(cholesky)/cholesky | solution.py:47
  403.8 11.8 %cholesky.110 = f32[127,127]{1,0:T(8,128)S(1)} custom-call(f32[127,127]{1,0:T(8,128)S(1)} %convolution_subtract_fusion.1), custom_call_target="Cholesky" | custom-call | tf_op jit(solution)/shard_map/jit(cholesky)/cholesky | solution.py:47
  418.5 19.7 %custom-call.15 = f32[2,128,128]{1,2,0:T(8,128)S(1)} custom-call(f32[2,128,128]{2,1,0:T(8,128)S(1)} %pad_maximum_fusion.15), custom_call_target="InvertDiagBlocksLowerTriangular" | custom-call | tf_op jit(solution)/shard_map/triangular_solve | solution.py:48
  440.4 3.2 fusion.31
  443.7 1.9 convolution_bitcast_fusion
  (179 shorter events, 46.7 us)
Async XLA Ops:
  7.2 15.1 %copy-start = (f32[16,64,128]{2,1,0:T(8,128)S(1)}, f32[16,64,128]{2,1,0:T(8,128)}, u32[]{:S(2)}) copy-start(f32[16,64,128]{2,1,0:T(8,128)} %param.13) | copy-start | bytes 1572868
  7.2 11.4 %copy-start.8 = (f32[8,4,64,256]{3,2,1,0:T(8,128)S(1)}, f32[8,4,64,256]{3,2,1,0:T(8,128)}, u32[]{:S(2)}) copy-start(f32[8,4,64,256]{3,2,1,0:T(8,128)} %param.10) | copy-start | bytes 6291460
  7.2 12.8 %copy-start.28 = (s32[1,1,64]{2,1,0:T(1,128)S(1)}, s32[1,1,64]{2,1,0:T(1,128)}, u32[]{:S(2)}) copy-start(s32[1,1,64]{2,1,0:T(1,128)} %param.15) | copy-start | bytes 772
  7.2 12.8 %copy-start.29 = (s32[1,1,64]{2,1,0:T(1,128)S(1)}, s32[1,1,64]{2,1,0:T(1,128)}, u32[]{:S(2)}) copy-start(s32[1,1,64]{2,1,0:T(1,128)} %param.16) | copy-start | bytes 772
  7.2 372.2 %all-reduce.4.cloned.1.call-start = ((), (), s32[]{:S(2)}) async-start(), calls=%async_computation | async-start | bytes 524288 | tf_op jit(solution)/shard_map/psum | solution.py:107
  9.7 25.5 %collective-permute-start.1 = (f32[8,1,64,256]{3,2,1,0:T(8,128)}, f32[8,1,64,256]{3,2,1,0:T(8,128)S(1)}, u32[]{:S(2)}, u32[]{:S(2)}) collective-permute-start(f32[8,1,64,256]{3,2,1,0:T(8,128)} %get-tuple-element.30), channel_id=1, source_target_pairs={{1,0},{2,1},{3,2},{4,3},{5,4},{6,5},{7,6},{8,7},{9,8},{10,9},{11,1... | collective-permute-start | bytes 1572872 | tf_op jit(solution)/shard_map/ppermute | solution.py:28
  13.0 9.1 %copy-start.27 = (f32[8,4]{0,1:T(4,128)S(1)}, f32[8,4]{0,1:T(4,128)}, u32[]{:S(2)}) copy-start(f32[8,4]{0,1:T(4,128)} %param.11) | copy-start | bytes 388
  13.0 22.1 %collective-permute-start.2 = (f32[8,1,64,256]{3,2,1,0:T(8,128)}, f32[8,1,64,256]{3,2,1,0:T(8,128)}, u32[]{:S(2)}, u32[]{:S(2)}) collective-permute-start(f32[8,1,64,256]{3,2,1,0:T(8,128)} %get-tuple-element.31), channel_id=1, source_target_pairs={{0,1},{1,2},{2,3},{3,4},{4,5},{5,6},{6,7},{7,8},{8,9},{9,10},{10,1... | collective-permute-start | bytes 1572872 | tf_op jit(solution)/shard_map/ppermute | solution.py:26
  19.3 15.9 %collective-permute-start = (f32[1,4,64,256]{3,2,1,0:T(8,128)}, f32[1,4,64,256]{3,2,1,0:T(8,128)S(1)}, u32[]{:S(2)}, u32[]{:S(2)}) collective-permute-start(f32[1,4,64,256]{3,2,1,0:T(8,128)} %slice.243), channel_id=1, source_target_pairs={{0,16},{16,32},{32,48},{48,64},{64,80},{80,96},{96,112},{112,0},{1... | collective-permute-start | bytes 786440 | tf_op jit(solution)/shard_map/ppermute | solution.py:15
  20.7 82.9 %copy-start.17 = (s32[6]{0:T(128)}, s32[6]{0:T(128)S(1)}, u32[]{:S(2)}) copy-start(s32[6]{0:T(128)S(1)} %iota_add_fusion) | copy-start | bytes 76
  20.7 82.8 %copy-start.20 = (pred[64]{0:T(512)(128)(4,1)}, pred[64]{0:T(512)(128)(4,1)S(1)}, u32[]{:S(2)}) copy-start(pred[64]{0:T(512)(128)(4,1)S(1)} %iota_compare_fusion.7) | copy-start | bytes 196
  22.2 2.0 copy-start.12
  22.2 13.0 %copy-start.13 = (f32[64]{0:T(128)S(1)}, f32[64]{0:T(128)}, u32[]{:S(2)}) copy-start(f32[64]{0:T(128)} %param.12) | copy-start | bytes 772
  39.5 31.3 %copy-start.4 = (f32[8,4,64,256]{3,2,1,0:T(8,128)}, f32[8,4,64,256]{3,2,1,0:T(8,128)S(1)}, u32[]{:S(2)}) copy-start(f32[8,4,64,256]{3,2,1,0:T(8,128)S(1)} %fusion.19) | copy-start | bytes 6291460
  41.5 40.0 %collective-permute-start.6 = (f32[8,1,64,256]{3,2,1,0:T(8,128)}, f32[8,1,64,256]{3,2,1,0:T(8,128)}, u32[]{:S(2)}, u32[]{:S(2)}) collective-permute-start(f32[8,1,64,256]{3,2,1,0:T(8,128)} %get-tuple-element.28), channel_id=1, source_target_pairs={{1,0},{2,1},{3,2},{4,3},{5,4},{6,5},{7,6},{8,7},{9,8},{10,9},{11,1... | collective-permute-start | bytes 1572872 | tf_op jit(solution)/shard_map/ppermute | solution.py:28
  43.4 38.1 %collective-permute-start.7 = (f32[8,1,64,256]{3,2,1,0:T(8,128)}, f32[8,1,64,256]{3,2,1,0:T(8,128)}, u32[]{:S(2)}, u32[]{:S(2)}) collective-permute-start(f32[8,1,64,256]{3,2,1,0:T(8,128)} %get-tuple-element.29), channel_id=1, source_target_pairs={{0,1},{1,2},{2,3},{3,4},{4,5},{5,6},{6,7},{7,8},{8,9},{9,10},{10,1... | collective-permute-start | bytes 1572872 | tf_op jit(solution)/shard_map/ppermute | solution.py:26
  48.6 32.9 %collective-permute-start.5 = (f32[1,4,64,256]{3,2,1,0:T(8,128)}, f32[1,4,64,256]{3,2,1,0:T(8,128)S(1)}, u32[]{:S(2)}, u32[]{:S(2)}) collective-permute-start(f32[1,4,64,256]{3,2,1,0:T(8,128)} %slice.336), channel_id=1, source_target_pairs={{0,16},{16,32},{32,48},{48,64},{64,80},{80,96},{96,112},{112,0},{1... | collective-permute-start | bytes 786440 | tf_op jit(solution)/shard_map/ppermute | solution.py:15
  63.0 4.8 %copy-start.14 = (s32[1,1,64]{2,1,0:T(1,128)S(1)}, s32[1,1,64]{2,1,0:T(1,128)}, u32[]{:S(2)}) copy-start(s32[1,1,64]{2,1,0:T(1,128)} %param.14) | copy-start | bytes 772
  73.3 45.6 %collective-permute-start.4 = (f32[1,256,256]{1,2,0:T(8,128)}, f32[1,256,256]{1,2,0:T(8,128)}, u32[]{:S(2)}, u32[]{:S(2)}) collective-permute-start(f32[1,256,256]{1,2,0:T(8,128)} %copy.72), channel_id=1, source_target_pairs={{1,0},{2,1},{3,2},{4,3},{5,4},{6,5},{7,6},{8,7},{9,8},{10,9},{11,1... | collective-permute-start | bytes 786440 | tf_op jit(solution)/shard_map/ppermute | solution.py:28
  76.3 49.0 %collective-permute-start.3 = (f32[1,256,256]{1,2,0:T(8,128)}, f32[1,256,256]{1,2,0:T(8,128)}, u32[]{:S(2)}, u32[]{:S(2)}) collective-permute-start(f32[1,256,256]{1,2,0:T(8,128)} %copy.70), channel_id=1, source_target_pairs={{0,1},{1,2},{2,3},{3,4},{4,5},{5,6},{6,7},{7,8},{8,9},{9,10},{10,1... | collective-permute-start | bytes 786440 | tf_op jit(solution)/shard_map/ppermute | solution.py:26
  107.8 21.6 %collective-permute-start.9 = (f32[1,256,256]{1,2,0:T(8,128)}, f32[1,256,256]{1,2,0:T(8,128)}, u32[]{:S(2)}, u32[]{:S(2)}) collective-permute-start(f32[1,256,256]{1,2,0:T(8,128)} %copy.77), channel_id=1, source_target_pairs={{1,0},{2,1},{3,2},{4,3},{5,4},{6,5},{7,6},{8,7},{9,8},{10,9},{11,1... | collective-permute-start | bytes 786440 | tf_op jit(solution)/shard_map/ppermute | solution.py:28
  110.7 19.7 %collective-permute-start.8 = (f32[1,256,256]{1,2,0:T(8,128)}, f32[1,256,256]{1,2,0:T(8,128)}, u32[]{:S(2)}, u32[]{:S(2)}) collective-permute-start(f32[1,256,256]{1,2,0:T(8,128)} %copy.75), channel_id=1, source_target_pairs={{0,1},{1,2},{2,3},{3,4},{4,5},{5,6},{6,7},{7,8},{8,9},{9,10},{10,1... | collective-permute-start | bytes 786440 | tf_op jit(solution)/shard_map/ppermute | solution.py:26
  117.0 23.2 %collective-permute-start.11 = (f32[8,1,64,256]{3,2,1,0:T(8,128)}, f32[8,1,64,256]{3,2,1,0:T(8,128)}, u32[]{:S(2)}, u32[]{:S(2)}) collective-permute-start(f32[8,1,64,256]{3,2,1,0:T(8,128)} %get-tuple-element.26), channel_id=1, source_target_pairs={{1,0},{2,1},{3,2},{4,3},{5,4},{6,5},{7,6},{8,7},{9,8},{10,9},{11,1... | collective-permute-start | bytes 1572872 | tf_op jit(solution)/shard_map/ppermute | solution.py:28
  118.9 21.3 %collective-permute-start.12 = (f32[8,1,64,256]{3,2,1,0:T(8,128)}, f32[8,1,64,256]{3,2,1,0:T(8,128)}, u32[]{:S(2)}, u32[]{:S(2)}) collective-permute-start(f32[8,1,64,256]{3,2,1,0:T(8,128)} %get-tuple-element.27), channel_id=1, source_target_pairs={{0,1},{1,2},{2,3},{3,4},{4,5},{5,6},{6,7},{7,8},{8,9},{9,10},{10,1... | collective-permute-start | bytes 1572872 | tf_op jit(solution)/shard_map/ppermute | solution.py:26
  127.2 13.0 %collective-permute-start.10 = (f32[1,4,64,256]{3,2,1,0:T(8,128)}, f32[1,4,64,256]{3,2,1,0:T(8,128)}, u32[]{:S(2)}, u32[]{:S(2)}) collective-permute-start(f32[1,4,64,256]{3,2,1,0:T(8,128)} %slice.345), channel_id=1, source_target_pairs={{0,16},{16,32},{32,48},{48,64},{64,80},{80,96},{96,112},{112,0},{1... | collective-permute-start | bytes 786440 | tf_op jit(solution)/shard_map/ppermute | solution.py:15
  145.3 4.5 copy-start.5
  159.2 4.8 %copy-start.15 = (s32[1,1,64]{2,1,0:T(1,128)S(1)}, s32[1,1,64]{2,1,0:T(1,128)}, u32[]{:S(2)}) copy-start(s32[1,1,64]{2,1,0:T(1,128)} %param.14) | copy-start | bytes 772
  159.2 4.8 %copy-start.18 = (s32[6]{0:T(128)S(1)}, s32[6]{0:T(128)}, u32[]{:S(2)}) copy-start(s32[6]{0:T(128)} %copy-done.17) | copy-start | bytes 76
  159.2 4.8 %copy-start.21 = (pred[64]{0:T(512)(128)(4,1)S(1)}, pred[64]{0:T(512)(128)(4,1)}, u32[]{:S(2)}) copy-start(pred[64]{0:T(512)(128)(4,1)} %copy-done.20) | copy-start | bytes 196
  164.0 12.4 %copy-start.3 = (f32[8,4,64,256]{3,2,1,0:T(8,128)S(1)}, f32[8,4,64,256]{3,2,1,0:T(8,128)}, u32[]{:S(2)}) copy-start(f32[8,4,64,256]{3,2,1,0:T(8,128)} %copy-done.2) | copy-start | bytes 6291460
  166.8 21.9 %collective-permute-start.16 = (f32[8,1,64,256]{3,2,1,0:T(8,128)}, f32[8,1,64,256]{3,2,1,0:T(8,128)}, u32[]{:S(2)}, u32[]{:S(2)}) collective-permute-start(f32[8,1,64,256]{3,2,1,0:T(8,128)} %get-tuple-element.24), channel_id=1, source_target_pairs={{1,0},{2,1},{3,2},{4,3},{5,4},{6,5},{7,6},{8,7},{9,8},{10,9},{11,1... | collective-permute-start | bytes 1572872 | tf_op jit(solution)/shard_map/ppermute | solution.py:28
  168.8 20.0 %collective-permute-start.17 = (f32[8,1,64,256]{3,2,1,0:T(8,128)}, f32[8,1,64,256]{3,2,1,0:T(8,128)}, u32[]{:S(2)}, u32[]{:S(2)}) collective-permute-start(f32[8,1,64,256]{3,2,1,0:T(8,128)} %get-tuple-element.25), channel_id=1, source_target_pairs={{0,1},{1,2},{2,3},{3,4},{4,5},{5,6},{6,7},{7,8},{8,9},{9,10},{10,1... | collective-permute-start | bytes 1572872 | tf_op jit(solution)/shard_map/ppermute | solution.py:26
  173.9 14.8 %collective-permute-start.15 = (f32[1,4,64,256]{3,2,1,0:T(8,128)}, f32[1,4,64,256]{3,2,1,0:T(8,128)}, u32[]{:S(2)}, u32[]{:S(2)}) collective-permute-start(f32[1,4,64,256]{3,2,1,0:T(8,128)} %slice.354), channel_id=1, source_target_pairs={{0,16},{16,32},{32,48},{48,64},{64,80},{80,96},{96,112},{112,0},{1... | collective-permute-start | bytes 786440 | tf_op jit(solution)/shard_map/ppermute | solution.py:15
  178.2 45.0 %collective-permute-start.14 = (f32[1,256,256]{1,2,0:T(8,128)S(1)}, f32[1,256,256]{1,2,0:T(8,128)}, u32[]{:S(2)}, u32[]{:S(2)}) collective-permute-start(f32[1,256,256]{1,2,0:T(8,128)S(1)} %copy.84), channel_id=1, source_target_pairs={{1,0},{2,1},{3,2},{4,3},{5,4},{6,5},{7,6},{8,7},{9,8},{10,9},{11,1... | collective-permute-start | bytes 786440 | tf_op jit(solution)/shard_map/ppermute | solution.py:28
  181.2 43.1 %collective-permute-start.13 = (f32[1,256,256]{1,2,0:T(8,128)}, f32[1,256,256]{1,2,0:T(8,128)}, u32[]{:S(2)}, u32[]{:S(2)}) collective-permute-start(f32[1,256,256]{1,2,0:T(8,128)} %copy.82), channel_id=1, source_target_pairs={{0,1},{1,2},{2,3},{3,4},{4,5},{5,6},{6,7},{7,8},{8,9},{9,10},{10,1... | collective-permute-start | bytes 786440 | tf_op jit(solution)/shard_map/ppermute | solution.py:26
  192.7 4.5 copy-start.6
  206.9 4.8 %copy-start.16 = (s32[1,1,64]{2,1,0:T(1,128)S(1)}, s32[1,1,64]{2,1,0:T(1,128)}, u32[]{:S(2)}) copy-start(s32[1,1,64]{2,1,0:T(1,128)} %param.14) | copy-start | bytes 772
  206.9 4.8 %copy-start.19 = (s32[6]{0:T(128)S(1)}, s32[6]{0:T(128)}, u32[]{:S(2)}) copy-start(s32[6]{0:T(128)} %copy-done.17) | copy-start | bytes 76
  206.9 4.8 %copy-start.22 = (pred[64]{0:T(512)(128)(4,1)S(1)}, pred[64]{0:T(512)(128)(4,1)}, u32[]{:S(2)}) copy-start(pred[64]{0:T(512)(128)(4,1)} %copy-done.20) | copy-start | bytes 196
  214.5 8.3 %copy-start.10 = (f32[8,128,64]{1,0,2:T(8,128)S(1)}, f32[8,128,64]{1,0,2:T(8,128)}, u32[]{:S(2)}) copy-start(f32[8,128,64]{1,0,2:T(8,128)} %add_add_fusion.2) | copy-start | bytes 786436
  214.5 8.3 %copy-start.25 = (f32[2,128]{1,0:T(2,128)S(1)}, f32[2,128]{1,0:T(2,128)}, u32[]{:S(2)}) copy-start(f32[2,128]{1,0:T(2,128)} %get-tuple-element.52) | copy-start | bytes 3076
  214.5 8.3 %copy-start.26 = (f32[2,128]{1,0:T(2,128)S(1)}, f32[2,128]{1,0:T(2,128)}, u32[]{:S(2)}) copy-start(f32[2,128]{1,0:T(2,128)} %get-tuple-element.53) | copy-start | bytes 3076
  215.2 10.5 %collective-permute-start.19 = (f32[1,256,256]{1,2,0:T(8,128)S(1)}, f32[1,256,256]{1,2,0:T(8,128)S(1)}, u32[]{:S(2)}, u32[]{:S(2)}) collective-permute-start(f32[1,256,256]{1,2,0:T(8,128)S(1)} %copy.90), channel_id=1, source_target_pairs={{1,0},{2,1},{3,2},{4,3},{5,4},{6,5},{7,6},{8,7},{9,8},{10,9},{11,1... | collective-permute-start | bytes 786440 | tf_op jit(solution)/shard_map/ppermute | solution.py:28
  217.5 8.4 %collective-permute-start.18 = (f32[1,256,256]{1,2,0:T(8,128)S(1)}, f32[1,256,256]{1,2,0:T(8,128)S(1)}, u32[]{:S(2)}, u32[]{:S(2)}) collective-permute-start(f32[1,256,256]{1,2,0:T(8,128)S(1)} %copy.88), channel_id=1, source_target_pairs={{0,1},{1,2},{2,3},{3,4},{4,5},{5,6},{6,7},{7,8},{8,9},{9,10},{10,1... | collective-permute-start | bytes 786440 | tf_op jit(solution)/shard_map/ppermute | solution.py:26
  229.9 188.5 %copy-start.11 = (f32[128,1]{1,0:T(8,128)S(1)}, f32[128,1]{1,0:T(8,128)}, u32[]{:S(2)}) copy-start(f32[128,1]{1,0:T(8,128)} %constant.108.clone.1) | copy-start | bytes 1540
  393.5 46.9 %copy-start.7 = (f32[8,4,64,256]{3,2,1,0:T(8,128)S(1)}, f32[8,4,64,256]{3,2,1,0:T(8,128)}, u32[]{:S(2)}) copy-start(f32[8,4,64,256]{3,2,1,0:T(8,128)} %fusion.4) | copy-start | bytes 6291460
  440.4 3.3 copy-start.9
  443.7 3.8 copy-start.1
  (3 other events, 3.6 us)
Sparse Core Ops, SparseCore 0:
  230.0 149.3 all-reduce.3

commit v2 on v1

v2 whole, which is shorter than its diff:
```python
import functools
import jax
import jax.numpy as jnp
from jax import lax
from jax.experimental import pallas as pl
from jax.experimental.pallas import tpu as pltpu
from jax.sharding import PartitionSpec as P

STEPS = 4
diffusion = 0.08
highest = lax.Precision.HIGHEST
MESH = pl.DeviceIdType.MESH
F32 = jnp.float32
BF16 = jnp.bfloat16

LON, LAT, ALT, WIDE = 8, 4, 64, 256
RAYS, SEG, TILES = 128, 16, 2
ROWS = TILES * RAYS
NEAR = 3 * TILES
PAIRS = LON * LAT // 2
HALF = 128
PACKED = WIDE + HALF


def state_mapping(gram_total):
    width_all = gram_total.shape[0]
    identity = jnp.eye(width_all - 1, dtype=jnp.float32)
    chol_lower = jnp.linalg.cholesky(identity + gram_total[1:, 1:])
    inverse = lax.linalg.triangular_solve(chol_lower, identity, left_side=True, lower=True)
    inner = jnp.dot(inverse, gram_total[1:, 0], precision=highest)
    weights = jnp.dot(inner, inverse, precision=highest)
    first_row = (jnp.arange(width_all) == 0).astype(jnp.float32)[None, :]
    lower_rows = jnp.concatenate([weights[:, None], inverse.T], axis=1)
    return jnp.concatenate([first_row, lower_rows], axis=0)


def split(x):
    high = x.astype(BF16)
    return high, (x - high.astype(F32)).astype(BF16)


def window_kernel(
    n_lon, n_lat,
    prior, courant, survival, geometry, near_key, path_key, observed, obs_weight,
    end_out, gram_out,
    s0, s1, s2, s3, s4, s_high, s_low, paths, counts, h_high, h_low,
    near, beside, gram, packed, got_lat, part, got_lon, total, decay,
    load_sem, store_sem, west_send, west_recv, row_send, row_recv,
    ray_send, ray_recv, lat_send, lat_recv, lon_send, lon_recv, all_send, all_recv,
):
    lon = lax.axis_index("lon")
    lat = lax.axis_index("lat")

    def at_lon(d):
        return (lax.rem(lon + d + n_lon, n_lon), lat)

    def at_lat(d):
        return (lon, lax.rem(lat + d + n_lat, n_lat))

    has_low = lat > 0
    has_high = lat < n_lat - 1
    states = [s0, s1, s2, s3]

    loads = pltpu.make_async_copy(prior, s0.at[1:LON + 1, 1:LAT + 1], load_sem)
    loads.start()

    barrier = pltpu.get_barrier_semaphore()
    for d in range(1, n_lon):
        pl.semaphore_signal(barrier, inc=1, device_id=at_lon(d), device_id_type=MESH)
    for d in range(1, n_lat):
        pl.semaphore_signal(barrier, inc=1, device_id=at_lat(d), device_id_type=MESH)
    pl.semaphore_wait(barrier, n_lon + n_lat - 2)

    def remote(src, dst, send, recv, to):
        return pltpu.make_async_remote_copy(
            src_ref=src, dst_ref=dst, send_sem=send, recv_sem=recv, device_id=to, device_id_type=MESH
        )

    def west_copy(k):
        src = prior.at[LON - 1] if k == 0 else states[k].at[LON, 1:LAT + 1]
        return remote(src, states[k].at[0, 1:LAT + 1], west_send.at[k], west_recv.at[k], at_lon(1))

    def up_copy(k):
        src = prior.at[:, LAT - 1] if k == 0 else states[k].at[1:LON + 1, LAT]
        return remote(src, states[k].at[1:LON + 1, 0], row_send.at[k, 0], row_recv.at[k, 0], at_lat(1))

    def down_copy(k):
        src = prior.at[:, 0] if k == 0 else states[k].at[1:LON + 1, 1]
        return remote(src, states[k].at[1:LON + 1, LAT + 1], row_send.at[k, 1], row_recv.at[k, 1], at_lat(-1))

    def ray_up(k):
        return remote(near.at[k, 2], beside.at[k, 0], ray_send.at[k, 0], ray_recv.at[k, 0], at_lat(1))

    def ray_down(k):
        return remote(near.at[k, 0], beside.at[k, 1], ray_send.at[k, 1], ray_recv.at[k, 1], at_lat(-1))

    def send_rows(k):
        @pl.when(has_high)
        def _():
            up_copy(k).start()

        @pl.when(has_low)
        def _():
            down_copy(k).start()

    def send_rays(k):
        @pl.when(has_high)
        def _():
            ray_up(k).start()

        @pl.when(has_low)
        def _():
            ray_down(k).start()

    send_rows(0)
    west_copy(0).start()

    @pl.when(jnp.logical_not(has_low))
    def _():
        for k in range(STEPS):
            def clear(i, c, k=k):
                states[k][i + 1, 0] = jnp.zeros((ALT, WIDE), F32)
                return c
            lax.fori_loop(0, LON, clear, 0)
            beside[k, 0] = jnp.zeros((ROWS, WIDE), F32)

    @pl.when(jnp.logical_not(has_high))
    def _():
        for k in range(STEPS):
            def clear(i, c, k=k):
                states[k][i + 1, LAT + 1] = jnp.zeros((ALT, WIDE), F32)
                return c
            lax.fori_loop(0, LON, clear, 0)
            beside[k, 1] = jnp.zeros((ROWS, WIDE), F32)

    decay[...] = jnp.broadcast_to(survival[...], (ALT, WIDE))

    def turn(s, c):
        block = geometry[s]
        paths[s] = jnp.concatenate([block, block], axis=0).T
        return c

    lax.fori_loop(0, SEG, turn, 0)
    slots = near_key.shape[1]
    left = (lax.broadcasted_iota(jnp.int32, (NEAR * PAIRS, slots), 0) == near_key[...]).astype(F32).astype(BF16)
    half = lax.broadcasted_iota(jnp.int32, (slots, HALF), 1) // ALT
    for s in range(SEG):
        right = (half + 2 * s == path_key[...]).astype(F32).astype(BF16)
        counts[:, s] = jnp.dot(left, right, preferred_element_type=F32)

    def build_tile(t, c):
        def build(p, c2):
            row = t * PAIRS + p
            number = counts[row]
            total_path = number[0:1] * paths[0]
            for s in range(1, SEG):
                total_path += number[s:s + 1] * paths[s]
            high, low = split(total_path)
            at = (pl.ds(pl.multiple_of(t * RAYS, RAYS), RAYS), pl.ds(pl.multiple_of(p * HALF, HALF), HALF))
            h_high[at] = high
            h_low[at] = low
            return c2

        return lax.fori_loop(0, PAIRS, build, c)

    lax.fori_loop(0, NEAR, build_tile, 0)
    gram[...] = jnp.zeros((WIDE, WIDE), F32)

    def cell(k, i, j):
        old = states[k]
        drift = courant[i, j]
        keep = 1.0 - 2.0 * diffusion - drift
        new = keep * old[i + 1, j + 1] + drift * old[i, j + 1]
        new += diffusion * (old[i + 1, j + 2] + old[i + 1, j])
        new = new * decay[...]
        if k + 1 < STEPS:
            states[k + 1][i + 1, j + 1] = new
        else:
            s4[i, j] = new
        high, low = split(new)
        at = pl.ds(pl.multiple_of((i * LAT + j) * ALT, ALT), ALT)
        s_high[at] = high
        s_low[at] = low

    def cells(k, first, rows):
        def one(i, c):
            for j in rows:
                cell(k, i, j)
            return c

        lax.fori_loop(first, LON, one, 0)

    def project(k):
        def part_of(b, c):
            at = pl.ds(pl.multiple_of(b * 256, 256), 256)
            high, low = s_high[at], s_low[at]
            add = jnp.dot(h_high[:, at], high, preferred_element_type=F32)
            add += jnp.dot(h_high[:, at], low, preferred_element_type=F32)
            add += jnp.dot(h_low[:, at], high, preferred_element_type=F32)
            add = add.reshape(3, ROWS, WIDE)

            @pl.when(b == 0)
            def _():
                near[k] = add

            @pl.when(b > 0)
            def _():
                near[k] += add

            return c

        lax.fori_loop(0, LON * LAT * ALT // 256, part_of, 0)

    def add_gram(k):
        @pl.when(has_low)
        def _():
            ray_up(k).wait_recv()

        @pl.when(has_high)
        def _():
            ray_down(k).wait_recv()

        rays = near[k, 1] + beside[k, 0] + beside[k, 1]
        lane = lax.broadcasted_iota(jnp.int32, (ROWS, WIDE), 1)
        rays = jnp.where(lane == 0, observed[:, k:k + 1] - rays, rays) * obs_weight[:, k:k + 1]
        gram[...] += jnp.dot(rays.T, rays, precision=highest, preferred_element_type=F32)

    loads.wait()
    for k in range(STEPS):
        cells(k, 1, range(1, LAT - 1))
        west_copy(k).wait_recv()
        for j in range(1, LAT - 1):
            cell(k, 0, j)

        @pl.when(has_low)
        def _(k=k):
            up_copy(k).wait_recv()

        @pl.when(has_high)
        def _(k=k):
            down_copy(k).wait_recv()

        cells(k, 0, (0, LAT - 1))
        if k + 1 < STEPS:
            send_rows(k + 1)
            west_copy(k + 1).start()
        else:
            ends = pltpu.make_async_copy(s4, end_out, store_sem)
            ends.start()
        project(k)
        send_rays(k)
        if k > 0:
            add_gram(k - 1)
    add_gram(STEPS - 1)

    packed[0:WIDE] = gram[:, 0:HALF]
    packed[WIDE:PACKED] = gram[HALF:WIDE, HALF:WIDE]
    piece = PACKED // n_lat

    def own(index):
        return pl.ds(pl.multiple_of(index * piece, 8), piece)

    def scatter(d):
        to = lax.rem(lat + d, n_lat)
        return remote(packed.at[own(to)], got_lat.at[d], lat_send.at[d], lat_recv.at[d], at_lat(d))

    def across(d):
        return remote(part, got_lon.at[d], lon_send.at[d], lon_recv.at[d], at_lon(d))

    def gather(d):
        return remote(total.at[own(lat)], total.at[own(lat)], all_send.at[d], all_recv.at[d], at_lat(d))

    def landed(d):
        back = lax.rem(lat - d + n_lat, n_lat)
        return remote(total.at[own(back)], total.at[own(back)], all_send.at[d], all_recv.at[d], at_lat(d))

    for d in range(1, n_lat):
        scatter(d).start()
    acc = packed[own(lat)]
    for d in range(1, n_lat):
        scatter(d).wait_recv()
        acc += got_lat[d]
    part[...] = acc
    for d in range(1, n_lon):
        across(d).start()
    for d in range(1, n_lon):
        across(d).wait_recv()
        acc += got_lon[d]
    total[own(lat)] = acc
    for d in range(1, n_lat):
        gather(d).start()
    for d in range(1, n_lat):
        landed(d).wait_recv()
    gram_out[...] = total[...]

    for k in range(STEPS):
        west_copy(k).wait_send()

        @pl.when(has_high)
        def _(k=k):
            up_copy(k).wait_send()
            ray_up(k).wait_send()

        @pl.when(has_low)
        def _(k=k):
            down_copy(k).wait_send()
            ray_down(k).wait_send()

    for d in range(1, n_lat):
        scatter(d).wait_send()
        gather(d).wait_send()
    for d in range(1, n_lon):
        across(d).wait_send()
    ends.wait()


def window(n_lon, n_lat, *operands):
    piece = PACKED // n_lat
    ghosts = pltpu.VMEM((LON + 1, LAT + 2, ALT, WIDE), F32)
    cells_all = LON * LAT * ALT
    vmem = pl.BlockSpec(memory_space=pltpu.VMEM)
    smem = pl.BlockSpec(memory_space=pltpu.SMEM)
    hbm = pl.BlockSpec(memory_space=pl.ANY)
    dma = pltpu.SemaphoreType.DMA
    return pl.pallas_call(
        functools.partial(window_kernel, n_lon, n_lat),
        out_shape=(
            jax.ShapeDtypeStruct((LON, LAT, ALT, WIDE), F32),
            jax.ShapeDtypeStruct((PACKED, HALF), F32),
        ),
        in_specs=[hbm, smem, vmem, vmem, vmem, vmem, vmem, vmem],
        out_specs=(hbm, vmem),
        scratch_shapes=[
            ghosts, ghosts, ghosts, ghosts,
            pltpu.VMEM((LON, LAT, ALT, WIDE), F32),
            pltpu.VMEM((cells_all, WIDE), BF16),
            pltpu.VMEM((cells_all, WIDE), BF16),
            pltpu.VMEM((SEG, RAYS, HALF), F32),
            pltpu.VMEM((NEAR * PAIRS, SEG, HALF), F32),
            pltpu.VMEM((NEAR * RAYS, cells_all), BF16),
            pltpu.VMEM((NEAR * RAYS, cells_all), BF16),
            pltpu.VMEM((STEPS, 3, ROWS, WIDE), F32),
            pltpu.VMEM((STEPS, 2, ROWS, WIDE), F32),
            pltpu.VMEM((WIDE, WIDE), F32),
            pltpu.VMEM((PACKED, HALF), F32),
            pltpu.VMEM((n_lat, piece, HALF), F32),
            pltpu.VMEM((piece, HALF), F32),
            pltpu.VMEM((n_lon, piece, HALF), F32),
            pltpu.VMEM((PACKED, HALF), F32),
            pltpu.VMEM((ALT, WIDE), F32),
            dma, dma,
            dma((STEPS,)), dma((STEPS,)),
            dma((STEPS, 2)), dma((STEPS, 2)),
            dma((STEPS, 2)), dma((STEPS, 2)),
            dma((n_lat,)), dma((n_lat,)),
            dma((n_lon,)), dma((n_lon,)),
            dma((n_lat,)), dma((n_lat,)),
        ],
        compiler_params=pltpu.CompilerParams(
            collective_id=0, has_side_effects=True, vmem_limit_bytes=56 * 1024 * 1024
        ),
        cost_estimate=pl.CostEstimate(flops=12_000_000_000, bytes_accessed=6_000_000, transcendentals=0),
        name="window",
    )(*operands)


def shards(
    prior_state,
    courant,
    cell_survival_rate,
    geometry,
    entry_tile,
    entry_column,
    entry_segment,
    entry_counts,
    observed,
    obs_weight,
):
    n_lon, n_lat = lax.axis_size("lon"), lax.axis_size("lat")
    tiles_here = entry_tile[0, 0]
    columns_here = entry_column[0, 0]
    slot_total = tiles_here.shape[0]
    live_slot = jnp.arange(slot_total, dtype=jnp.int32) < entry_counts[0, 0]
    near_tile = tiles_here - (lax.axis_index("lat") - 1) * TILES
    near_key = jnp.where(live_slot, near_tile * PAIRS + columns_here // 2, -1)[None, :]
    path_key = (entry_segment[0, 0] * 2 + columns_here % 2)[:, None]
    end_forecast, packed = window(
        n_lon, n_lat,
        prior_state, courant, cell_survival_rate[:, None], geometry, near_key, path_key,
        observed.reshape(STEPS, ROWS).T, obs_weight.reshape(STEPS, ROWS).T,
    )
    upper = packed[HALF:WIDE].T
    gram_total = jnp.concatenate(
        [packed[:WIDE], jnp.concatenate([upper, packed[WIDE:]], axis=0)], axis=1
    )
    update = state_mapping(gram_total)
    end_state = jnp.dot(
        end_forecast.reshape(-1, WIDE), update, precision=highest
    ).reshape(prior_state.shape)
    start_state = jnp.dot(
        prior_state.reshape(-1, WIDE), update, precision=highest
    ).reshape(prior_state.shape)
    return (start_state, end_state)


def solution(mesh):
    placed = (
        P("lon", "lat", None, None),
        P("lon", "lat"),
        P(),
        P(),
        P("lon", "lat", None),
        P("lon", "lat", None),
        P("lon", "lat", None),
        P("lon", "lat"),
        P(None, "lon", "lat", None),
        P(None, "lon", "lat", None),
    )
    return jax.shard_map(
        shards,
        mesh=mesh,
        in_specs=placed,
        out_specs=(P("lon", "lat", None, None), P("lon", "lat", None, None)),
        check_vma=False,
    )
```

time: 461 us -> 213 us (0.46); the launches traced: 454 us -> 212 us
  waiting for transfers between devices: 170 us -> 0 us
  Pallas kernels: 0 us -> 134 us
  starting transfers between devices: 63.8 us -> 0 us
  local copies, waits for them, and re-layouts: 68.2 us -> 11.4 us
  matrix products: 60.1 us -> 7.12 us
  other arithmetic: 74.7 us -> 57.4 us
  between operations: 17.3 us -> 2.8 us
    psum x1 -> x0, waiting for transfers between devices: 149 us -> none  [shards(): gram_total = lax.psum(gram_local, ('lon', 'lat'))]
    pallas_call x0 -> x1, Pallas kernels: none -> 134 us  [window(): pl.pallas_call(functools.partial(window_kernel, n_lon, n_lat), out_shape=...]
    ppermute x20 -> x0, starting transfers between devices: 63.8 us -> none  [the longest x8 41.7 us: extended(): lax.ppermute(tail, axis, [(i, (i + 1) % count) for i in range(ends)])]
    dot_general x14 -> x2, matrix products: 57.4 us -> 5.17 us  [the longest x1 3.22 us: shards(): jnp.dot(end_forecast.reshape(-1, WIDE), update, precision=highest)]
    ppermute x20 -> x0, waiting for transfers between devices: 20.9 us -> none  [the longest x4 20.7 us: from_behind(): lax.ppermute(x, axis, [(i, (i + by) % devices) for i in range(devices)])]
    slice x32 -> x3, local copies, waits for them, and re-layouts: 21.9 us -> 1.03 us  [the longest x1 1.01 us: state_mapping(): inner = jnp.dot(inverse, gram_total[1:, 0], precision=highest)]
    gather x5 -> x0, local copies, waits for them, and re-layouts: 16.6 us -> none  [the longest x4 14.6 us: shards(): current_state.reshape(lon_cells * lat_cells, alt_cells, width_all)]
    mul x7 -> x1, other arithmetic: 16.6 us -> 0.66 us  [shards(): path_key = (entry_segment[0, 0] * 2 + columns_here % 2)[:, None]]
  transfers between devices with their start and end apart: 21 -> 0, of which waited for: 5 -> 0; matrix products, arithmetic and copies ran while one was open for 21% -> 0% of each run, Pallas kernels for 0% -> 0%
where the time goes in v2:
time: 213 us; the launch traced here: 212 us
  Pallas kernels  134 us (63%)
  other arithmetic  57.4 us (27%)
  local copies, waits for them, and re-layouts  11.4 us (5%)
  matrix products  7.12 us (3%)
  between operations  2.8 us (1%)
    pallas_call x1, Pallas kernels, window(): pl.pallas_call(functools.partial(window_kernel, n_lon, n_lat), out_shape=...  134 us
    another operation x7, other arithmetic, state_mapping(): chol_lower = jnp.linalg.cholesky(identity + gram_total[1:, 1:])  34.7 us
    another operation x4, other arithmetic, state_mapping(): lax.linalg.triangular_solve(chol_lower, identity, left_side=True, lower=T...  19.8 us
    unnamed x9, local copies, waits for them, and re-layouts  4.33 us

profile of v2, /device:TPU:1, one launch (start us, length us, event | category | flops | bytes accessed | tf_op | source)
XLA Modules:
  0.0 212.3 jit_solution(980354930521467543)
XLA Ops:
  1.3 1.2 compare_select_fusion.near_key
  2.5 0.7 multiply_bitcast_fusion
  3.1 1.3 copy.31.courant
  4.5 0.1 copy.28
  4.6 1.3 copy.32.survival
  5.9 0.7 copy.25
  6.7 0.6 fusion.16.path_key
  7.3 1.5 copy.29
  8.8 1.5 copy.30
  10.3 133.6 %window.1 = (f32[8,4,64,256]{3,2,1,0:T(8,128)}, f32[384,128]{1,0:T(8,128)}) custom-call(f32[8,4,64,256]{3,2,1,0:T(8,128)} %prior.1, f32[8,4]{1,0:T(8,128)} %copy.31.courant, f32[64,1]{1,0:T(8,128)} %copy.32.survival, f32[16,64,128]{2,1,0:T(8,128)} %geometry.1, s32[1,64]{1,0:T(1,128)} %compare_select_fusion.near_key, s32[64,1]{1,0:T(8,128)} %fusion.16.path_key, ...), custom_call_target="tpu_custom_call" | custom-call | flops 12000000000 | bytes 6000000 | tf_op jit(solution)/shard_map/window/pallas_call | solution.py:325
  143.9 1.0 slice_reduce_fusion
  144.9 0.9 slice_bitcast_fusion.5
  145.8 1.1 copy.33
  146.8 0.0 copy-start.2
  146.9 0.2 fusion
  147.0 0.1 copy.35
  147.2 0.2 fusion.3
  147.4 11.7 %cholesky.51 = f32[128,128]{1,0:T(8,128)S(1)} custom-call(f32[128,128]{1,0:T(8,128)S(1)} %cholesky.124), custom_call_target="Cholesky" | custom-call | tf_op jit(solution)/shard_map/jit(cholesky)/cholesky | solution.py:28
  159.1 0.6 compare_reduce_fusion.1
  159.7 9.8 %custom-call.14 = f32[1,128,128]{1,2,0:T(8,128)S(1)} custom-call(f32[1,128,128]{2,1,0:T(8,128)S(1)} %get-tuple-element.31), custom_call_target="InvertDiagBlocksLowerTriangular" | custom-call | tf_op jit(solution)/shard_map/jit(cholesky)/cholesky | solution.py:28
  169.6 0.0 copy-start.1
  169.6 0.2 constant_dynamic-update-slice_fusion.1
  169.8 0.3 convolution_subtract_fusion.1
  170.1 11.8 %cholesky.110 = f32[127,127]{1,0:T(8,128)S(1)} custom-call(f32[127,127]{1,0:T(8,128)S(1)} %convolution_subtract_fusion.1), custom_call_target="Cholesky" | custom-call | tf_op jit(solution)/shard_map/jit(cholesky)/cholesky | solution.py:28
  181.9 0.6 compare_reduce_fusion
  183.9 0.0 copy-done.2
  183.9 0.1 fusion.11
  184.0 19.7 %custom-call.15 = f32[2,128,128]{1,2,0:T(8,128)S(1)} custom-call(f32[2,128,128]{2,1,0:T(8,128)S(1)} %pad_maximum_fusion.5), custom_call_target="InvertDiagBlocksLowerTriangular" | custom-call | tf_op jit(solution)/shard_map/triangular_solve | solution.py:29
  203.7 0.3 fusion.6
  204.0 0.4 convolution_subtract_fusion
  204.4 0.3 fusion.10
  204.7 0.3 convolution_bitcast_fusion.2
  204.9 0.3 convolution_bitcast_fusion.1
  205.2 0.1 fusion.4
  205.3 0.0 copy-done.1
  205.3 0.0 copy-start
  205.3 3.2 %fusion.1 = f32[8,4,64,256]{3,2,1,0:T(8,128)} fusion(f32[8,4,64,256]{3,2,1,0:T(8,128)S(1)} %copy-done.1, f32[255,255]{0,1:T(8,128)S(1)} %fusion.4, f32[255,1]{0,1:T(1,128)S(1)} %convolution_bitcast_fusion.1, f32[1,256]{0,1:T(8,128)S(1)} %fusion.5), kind=kOutput, calls=%fused_computation.11 | convolution fusion | flops 1610743808 | bytes 4456448 | tf_op jit(solution)/shard_map/dot_general | solution.py:397
  208.5 0.0 copy-done
  208.5 1.9 convolution_bitcast_fusion
  210.5 1.8 copy.36
  (12 shorter events, 0.2 us)
Async XLA Ops:
  146.8 37.1 %copy-start.2 = (f32[128,1]{1,0:T(8,128)S(1)}, f32[128,1]{1,0:T(8,128)}, u32[]{:S(2)}) copy-start(f32[128,1]{1,0:T(8,128)} %constant.125.clone.1) | copy-start | bytes 1540
  169.6 35.7 %copy-start.1 = (f32[8,4,64,256]{3,2,1,0:T(8,128)S(1)}, f32[8,4,64,256]{3,2,1,0:T(8,128)}, u32[]{:S(2)}) copy-start(f32[8,4,64,256]{3,2,1,0:T(8,128)} %get-tuple-element.5) | copy-start | bytes 6291460
  205.3 3.2 %copy-start = (f32[8,4,64,256]{3,2,1,0:T(8,128)S(1)}, f32[8,4,64,256]{3,2,1,0:T(8,128)}, u32[]{:S(2)}) copy-start(f32[8,4,64,256]{3,2,1,0:T(8,128)} %prior.1) | copy-start | bytes 6291460

commit v3 on v2

--- a/solution.py
+++ b/solution.py
@@ -20,18 +20,9 @@
 PAIRS = LON * LAT // 2
 HALF = 128
 PACKED = WIDE + HALF
-
-
-def state_mapping(gram_total):
-    width_all = gram_total.shape[0]
-    identity = jnp.eye(width_all - 1, dtype=jnp.float32)
-    chol_lower = jnp.linalg.cholesky(identity + gram_total[1:, 1:])
-    inverse = lax.linalg.triangular_solve(chol_lower, identity, left_side=True, lower=True)
-    inner = jnp.dot(inverse, gram_total[1:, 0], precision=highest)
-    weights = jnp.dot(inner, inverse, precision=highest)
-    first_row = (jnp.arange(width_all) == 0).astype(jnp.float32)[None, :]
-    lower_rows = jnp.concatenate([weights[:, None], inverse.T], axis=1)
-    return jnp.concatenate([first_row, lower_rows], axis=0)
+PANEL = 16
+CELLS = LON * LAT * ALT
+CHUNKS = 8
 
 
 def split(x):
@@ -41,10 +32,11 @@
 
 def window_kernel(
     n_lon, n_lat,
-    prior, courant, survival, geometry, near_key, path_key, observed, obs_weight,
-    end_out, gram_out,
-    s0, s1, s2, s3, s4, s_high, s_low, paths, counts, h_high, h_low,
-    near, beside, gram, packed, got_lat, part, got_lon, total, decay,
+    prior, courant, survival, geometry, entry_tile, entry_column, entry_segment, entry_counts,
+    observed, obs_weight,
+    prior_high, prior_low, end_high, end_low, gram_out,
+    s0, s1, s2, s3, p_high, p_low, s_high, s_low, paths, counts, h_high, h_low,
+    near, beside, gram, packed, got_lat, part, got_lon, total, decay, drifts, seen, scales,
     load_sem, store_sem, west_send, west_recv, row_send, row_recv,
     ray_send, ray_recv, lat_send, lat_recv, lon_send, lon_recv, all_send, all_recv,
 ):
@@ -133,7 +125,20 @@
             lax.fori_loop(0, LON, clear, 0)
             beside[k, 1] = jnp.zeros((ROWS, WIDE), F32)
 
-    decay[...] = jnp.broadcast_to(survival[...], (ALT, WIDE))
+    def upright(line):
+        return jnp.broadcast_to(line, (HALF, HALF)).T
+
+    line = survival[...]
+    line = upright(jnp.concatenate([line, line], axis=1))[0:ALT]
+    decay[...] = jnp.concatenate([line, line], axis=1)
+    for j in range(LAT):
+        column = jnp.broadcast_to(courant[:, j:j + 1], (LON, WIDE))
+        for i in range(LON):
+            drifts[i, j] = jnp.broadcast_to(column[i:i + 1], (8, WIDE))
+    for k in range(STEPS):
+        for t in range(TILES):
+            seen[k, t * RAYS:(t + 1) * RAYS] = upright(observed[k, 0, t:t + 1])
+            scales[k, t * RAYS:(t + 1) * RAYS] = upright(obs_weight[k, 0, t:t + 1])
 
     def turn(s, c):
         block = geometry[s]
@@ -141,12 +146,19 @@
         return c
 
     lax.fori_loop(0, SEG, turn, 0)
-    slots = near_key.shape[1]
-    left = (lax.broadcasted_iota(jnp.int32, (NEAR * PAIRS, slots), 0) == near_key[...]).astype(F32).astype(BF16)
-    half = lax.broadcasted_iota(jnp.int32, (slots, HALF), 1) // ALT
+    slots = entry_tile.shape[2]
+    column = entry_column[0]
+    live = lax.broadcasted_iota(jnp.int32, (1, slots), 1) < entry_counts[...]
+    near_key = (entry_tile[0] - (lat - 1) * TILES) * PAIRS + column // 2
+    near_key = jnp.where(live, near_key, -1)
+    path_key = entry_segment[0] * 2 + column % 2
+    left = (lax.broadcasted_iota(jnp.int32, (NEAR * PAIRS, slots), 0) == near_key).astype(F32).astype(BF16)
+    half = lax.broadcasted_iota(jnp.int32, (HALF, slots), 0) // ALT
     for s in range(SEG):
-        right = (half + 2 * s == path_key[...]).astype(F32).astype(BF16)
-        counts[:, s] = jnp.dot(left, right, preferred_element_type=F32)
+        right = (half + 2 * s == path_key).astype(F32).astype(BF16)
+        counts[:, s] = lax.dot_general(
+            left, right, (((1,), (1,)), ((), ())), preferred_element_type=F32
+        )
 
     def build_tile(t, c):
         def build(p, c2):
@@ -168,15 +180,13 @@
 
     def cell(k, i, j):
         old = states[k]
-        drift = courant[i, j]
+        drift = drifts[i, j, 0:1]
         keep = 1.0 - 2.0 * diffusion - drift
         new = keep * old[i + 1, j + 1] + drift * old[i, j + 1]
         new += diffusion * (old[i + 1, j + 2] + old[i + 1, j])
         new = new * decay[...]
         if k + 1 < STEPS:
             states[k + 1][i + 1, j + 1] = new
-        else:
-            s4[i, j] = new
         high, low = split(new)
         at = pl.ds(pl.multiple_of((i * LAT + j) * ALT, ALT), ALT)
         s_high[at] = high
@@ -222,10 +232,28 @@
 
         rays = near[k, 1] + beside[k, 0] + beside[k, 1]
         lane = lax.broadcasted_iota(jnp.int32, (ROWS, WIDE), 1)
-        rays = jnp.where(lane == 0, observed[:, k:k + 1] - rays, rays) * obs_weight[:, k:k + 1]
+        rays = jnp.where(lane == 0, jnp.concatenate([seen[k], seen[k]], axis=1) - rays, rays)
+        rays = rays * jnp.concatenate([scales[k], scales[k]], axis=1)
         gram[...] += jnp.dot(rays.T, rays, precision=highest, preferred_element_type=F32)
 
     loads.wait()
+
+    def split_prior(i, c):
+        high, low = split(s0[i + 1, 1:LAT + 1].reshape(LAT * ALT, WIDE))
+        at = pl.ds(pl.multiple_of(i * LAT * ALT, LAT * ALT), LAT * ALT)
+        p_high[at] = high
+        p_low[at] = low
+        return c
+
+    lax.fori_loop(0, LON, split_prior, 0)
+    stores = [
+        pltpu.make_async_copy(src, dst, store_sem.at[n])
+        for n, (src, dst) in enumerate(
+            ((p_high, prior_high), (p_low, prior_low), (s_high, end_high), (s_low, end_low))
+        )
+    ]
+    for copy in stores[:2]:
+        copy.start()
     for k in range(STEPS):
         cells(k, 1, range(1, LAT - 1))
         west_copy(k).wait_recv()
@@ -245,8 +273,8 @@
             send_rows(k + 1)
             west_copy(k + 1).start()
         else:
-            ends = pltpu.make_async_copy(s4, end_out, store_sem)
-            ends.start()
+            for copy in stores[2:]:
+                copy.start()
         project(k)
         send_rays(k)
         if k > 0:
@@ -311,34 +339,35 @@
         gather(d).wait_send()
     for d in range(1, n_lon):
         across(d).wait_send()
-    ends.wait()
+    for copy in stores:
+        copy.wait()
 
 
 def window(n_lon, n_lat, *operands):
     piece = PACKED // n_lat
     ghosts = pltpu.VMEM((LON + 1, LAT + 2, ALT, WIDE), F32)
-    cells_all = LON * LAT * ALT
+    half_type = jax.ShapeDtypeStruct((CELLS, WIDE), BF16)
     vmem = pl.BlockSpec(memory_space=pltpu.VMEM)
-    smem = pl.BlockSpec(memory_space=pltpu.SMEM)
     hbm = pl.BlockSpec(memory_space=pl.ANY)
     dma = pltpu.SemaphoreType.DMA
     return pl.pallas_call(
         functools.partial(window_kernel, n_lon, n_lat),
         out_shape=(
-            jax.ShapeDtypeStruct((LON, LAT, ALT, WIDE), F32),
+            half_type, half_type, half_type, half_type,
             jax.ShapeDtypeStruct((PACKED, HALF), F32),
         ),
-        in_specs=[hbm, smem, vmem, vmem, vmem, vmem, vmem, vmem],
-        out_specs=(hbm, vmem),
+        in_specs=[hbm] + [vmem] * 9,
+        out_specs=(hbm, hbm, hbm, hbm, vmem),
         scratch_shapes=[
             ghosts, ghosts, ghosts, ghosts,
-            pltpu.VMEM((LON, LAT, ALT, WIDE), F32),
-            pltpu.VMEM((cells_all, WIDE), BF16),
-            pltpu.VMEM((cells_all, WIDE), BF16),
+            pltpu.VMEM((CELLS, WIDE), BF16),
+            pltpu.VMEM((CELLS, WIDE), BF16),
+            pltpu.VMEM((CELLS, WIDE), BF16),
+            pltpu.VMEM((CELLS, WIDE), BF16),
             pltpu.VMEM((SEG, RAYS, HALF), F32),
             pltpu.VMEM((NEAR * PAIRS, SEG, HALF), F32),
-            pltpu.VMEM((NEAR * RAYS, cells_all), BF16),
-            pltpu.VMEM((NEAR * RAYS, cells_all), BF16),
+            pltpu.VMEM((NEAR * RAYS, CELLS), BF16),
+            pltpu.VMEM((NEAR * RAYS, CELLS), BF16),
             pltpu.VMEM((STEPS, 3, ROWS, WIDE), F32),
             pltpu.VMEM((STEPS, 2, ROWS, WIDE), F32),
             pltpu.VMEM((WIDE, WIDE), F32),
@@ -348,7 +377,10 @@
             pltpu.VMEM((n_lon, piece, HALF), F32),
             pltpu.VMEM((PACKED, HALF), F32),
             pltpu.VMEM((ALT, WIDE), F32),
-            dma, dma,
+            pltpu.VMEM((LON, LAT, 8, WIDE), F32),
+            pltpu.VMEM((STEPS, ROWS, HALF), F32),
+            pltpu.VMEM((STEPS, ROWS, HALF), F32),
+            dma, dma((4,)),
             dma((STEPS,)), dma((STEPS,)),
             dma((STEPS, 2)), dma((STEPS, 2)),
             dma((STEPS, 2)), dma((STEPS, 2)),
@@ -364,6 +396,145 @@
     )(*operands)
 
 
+def panel_rows(block, at, rows_low, rows_high):
+    spread = {}
+    for j in range(PANEL):
+        column = jnp.broadcast_to(block[:, at + j:at + j + 1], (PANEL, HALF))
+        for i in range(j, PANEL):
+            spread[i, j] = jnp.broadcast_to(column[i:i + 1], (8, HALF))
+    rows = [
+        [jnp.broadcast_to(part[i:i + 1], (8, HALF)) for part in (rows_low, rows_high)]
+        for i in range(PANEL)
+    ]
+    for k in range(PANEL):
+        scale = lax.rsqrt(spread[k, k])
+        for i in range(k + 1, PANEL):
+            spread[i, k] = spread[i, k] * scale
+        rows[k] = [part * scale for part in rows[k]]
+        for i in range(k + 1, PANEL):
+            factor = spread[i, k]
+            for j in range(k + 1, i + 1):
+                spread[i, j] = spread[i, j] - factor * spread[j, k]
+            rows[i] = [a - factor * b for a, b in zip(rows[i], rows[k])]
+    return rows
+
+
+def update_kernel(packed, prior_high, prior_low, end_high, end_low, start_out, end_out,
+                  work, inverse, panel, u_high, u_low, z, results, load_sem, store_sem):
+    sources = (prior_high, prior_low, end_high, end_low)
+    loads = [pltpu.make_async_copy(src, z.at[n], load_sem.at[n]) for n, src in enumerate(sources)]
+    for copy in loads:
+        copy.start()
+
+    lower = packed[0:WIDE]
+    corner = lower[HALF:WIDE].T
+    row = lax.broadcasted_iota(jnp.int32, (HALF, HALF), 0)
+    lane = lax.broadcasted_iota(jnp.int32, (HALF, HALF), 1)
+    same = (row == lane).astype(F32)
+    inner = jnp.logical_and(row > 0, lane > 0)
+    work[0:HALF, 0:HALF] = jnp.where(inner, lower[0:HALF], 0.0) + same
+    work[0:HALF, HALF:WIDE] = jnp.where(row > 0, corner, 0.0)
+    work[HALF:WIDE, 0:HALF] = jnp.where(lane > 0, lower[HALF:WIDE], 0.0)
+    work[HALF:WIDE, HALF:WIDE] = packed[WIDE:PACKED] + same
+
+    for p in range(WIDE // PANEL):
+        first = p * PANEL
+        side, at = first // HALF, first % HALF
+        mine = slice(first, first + PANEL)
+        lanes = lax.broadcasted_iota(jnp.int32, (PANEL, HALF), 1)
+        rows_of = lax.broadcasted_iota(jnp.int32, (PANEL, HALF), 0)
+        parts = [work[mine, 0:HALF], work[mine, HALF:WIDE]]
+        block = parts[side]
+        in_panel = jnp.logical_and(lanes >= at, lanes < at + PANEL)
+        unit = (lanes == rows_of + at).astype(F32)
+        if p == 0:
+            right = jnp.logical_and(lanes == 0, rows_of > 0)
+            unit = jnp.where(right, lower[mine], unit)
+        parts[side] = jnp.where(in_panel, unit, block)
+        rows = panel_rows(block, at, *parts)
+        for i in range(PANEL):
+            for h in range(2):
+                panel[i:i + 1, h * HALF:(h + 1) * HALF] = rows[i][h][0:1]
+        done = panel[...]
+        wide = lax.broadcasted_iota(jnp.int32, (PANEL, WIDE), 1)
+        inverse[mine] = jnp.where(wide < first + PANEL, done, 0.0)
+        rest = first + PANEL
+        if rest == WIDE:
+            break
+        high, low = split(done)
+        left = jnp.concatenate([high, high, low], axis=0)
+        both = jnp.concatenate([high, low, high], axis=0)
+        begin = HALF if rest >= HALF else 0
+        change = lax.dot_general(
+            left[:, begin:], both, (((0,), (0,)), ((), ())), preferred_element_type=F32
+        )
+        old = work[rest:WIDE]
+        wide = lax.broadcasted_iota(jnp.int32, (WIDE - rest, WIDE), 1)
+        blank = jnp.logical_and(wide >= first, wide < rest)
+        if p == 0:
+            start = jnp.where(lane[0:1] == 0, lower[rest:WIDE], 0.0)
+            start = jnp.concatenate([start, jnp.zeros_like(start)], axis=1)
+            old = jnp.where(blank, start, old)
+        else:
+            old = jnp.where(blank, 0.0, old)
+        work[rest:WIDE] = old - change[rest - begin:]
+
+    whole = inverse[...]
+    wide = lax.broadcasted_iota(jnp.int32, (WIDE, WIDE), 1)
+    tall = lax.broadcasted_iota(jnp.int32, (WIDE, WIDE), 0)
+    right = jnp.where(tall[:, 0:1] > 0, whole[:, 0:1], 0.0)
+    whole = jnp.where(jnp.logical_and(wide == 0, tall > 0), 0.0, whole)
+    weights = jnp.sum(right * whole, axis=0, keepdims=True)
+    turned = jnp.where(tall == 0, whole + weights, whole)
+    high, low = split(turned.T)
+    u_high[...] = high
+    u_low[...] = low
+
+    for copy in loads:
+        copy.wait()
+    size = CELLS // CHUNKS
+    stores = []
+    for n, out in enumerate((start_out, end_out)):
+        for b in range(CHUNKS):
+            at = slice(b * size, (b + 1) * size)
+            a_high, a_low = z[2 * n, at], z[2 * n + 1, at]
+            value = jnp.dot(a_high, u_high[...], preferred_element_type=F32)
+            value += jnp.dot(a_low, u_high[...], preferred_element_type=F32)
+            value += jnp.dot(a_high, u_low[...], preferred_element_type=F32)
+            results[n, at] = value
+            copy = pltpu.make_async_copy(results.at[n, at], out.at[at], store_sem.at[n, b])
+            copy.start()
+            stores.append(copy)
+    for copy in stores:
+        copy.wait()
+
+
+def apply_update(packed, prior_high, prior_low, end_high, end_low):
+    vmem = pl.BlockSpec(memory_space=pltpu.VMEM)
+    hbm = pl.BlockSpec(memory_space=pl.ANY)
+    out = jax.ShapeDtypeStruct((CELLS, WIDE), F32)
+    return pl.pallas_call(
+        update_kernel,
+        out_shape=(out, out),
+        in_specs=[vmem, hbm, hbm, hbm, hbm],
+        out_specs=(hbm, hbm),
+        scratch_shapes=[
+            pltpu.VMEM((WIDE, WIDE), F32),
+            pltpu.VMEM((WIDE, WIDE), F32),
+            pltpu.VMEM((PANEL, WIDE), F32),
+            pltpu.VMEM((WIDE, WIDE), BF16),
+            pltpu.VMEM((WIDE, WIDE), BF16),
+            pltpu.VMEM((4, CELLS, WIDE), BF16),
+            pltpu.VMEM((2, CELLS, WIDE), F32),
+            pltpu.SemaphoreType.DMA((4,)),
+            pltpu.SemaphoreType.DMA((2, CHUNKS)),
+        ],
+        compiler_params=pltpu.CompilerParams(vmem_limit_bytes=60 * 1024 * 1024),
+        cost_estimate=pl.CostEstimate(flops=1_700_000_000, bytes_accessed=8_400_000, transcendentals=0),
+        name="update",
+    )(packed, prior_high, prior_low, end_high, end_low)
+
+
 def shards(
     prior_state,
     courant,
@@ -377,30 +548,13 @@
     obs_weight,
 ):
     n_lon, n_lat = lax.axis_size("lon"), lax.axis_size("lat")
-    tiles_here = entry_tile[0, 0]
-    columns_here = entry_column[0, 0]
-    slot_total = tiles_here.shape[0]
-    live_slot = jnp.arange(slot_total, dtype=jnp.int32) < entry_counts[0, 0]
-    near_tile = tiles_here - (lax.axis_index("lat") - 1) * TILES
-    near_key = jnp.where(live_slot, near_tile * PAIRS + columns_here // 2, -1)[None, :]
-    path_key = (entry_segment[0, 0] * 2 + columns_here % 2)[:, None]
-    end_forecast, packed = window(
+    prior_high, prior_low, end_high, end_low, packed = window(
         n_lon, n_lat,
-        prior_state, courant, cell_survival_rate[:, None], geometry, near_key, path_key,
-        observed.reshape(STEPS, ROWS).T, obs_weight.reshape(STEPS, ROWS).T,
+        prior_state, courant, cell_survival_rate[None, :], geometry,
+        entry_tile, entry_column, entry_segment, entry_counts, observed, obs_weight,
     )
-    upper = packed[HALF:WIDE].T
-    gram_total = jnp.concatenate(
-        [packed[:WIDE], jnp.concatenate([upper, packed[WIDE:]], axis=0)], axis=1
-    )
-    update = state_mapping(gram_total)
-    end_state = jnp.dot(
-        end_forecast.reshape(-1, WIDE), update, precision=highest
-    ).reshape(prior_state.shape)
-    start_state = jnp.dot(
-        prior_state.reshape(-1, WIDE), update, precision=highest
-    ).reshape(prior_state.shape)
-    return (start_state, end_state)
+    start_state, end_state = apply_update(packed, prior_high, prior_low, end_high, end_low)
+    return (start_state.reshape(prior_state.shape), end_state.reshape(prior_state.shape))
 
 
 def solution(mesh):

time: 213 us -> 155 us (0.73)
  other arithmetic: 57.4 us -> 0 us
  Pallas kernels: 134 us -> 152 us
  local copies, waits for them, and re-layouts: 11.4 us -> 1.35 us
  matrix products: 7.12 us -> 0 us
    another operation x11 -> x0, other arithmetic: 54.5 us -> none  [the longest x7 34.7 us: state_mapping(): chol_lower = jnp.linalg.cholesky(identity + gram_total[1:, 1:])]
    pallas_call x0 -> x1, Pallas kernels: none -> 16.2 us  [apply_update(): pl.pallas_call(update_kernel, out_shape=(out, out), in_specs=[vmem, hbm,...]
    dot_general x4 -> x0, matrix products: 5.69 us -> none  [the longest x1 3.22 us: shards(): jnp.dot(end_forecast.reshape(-1, WIDE), update, precision=highest)]
    unnamed x9 -> x1, local copies, waits for them, and re-layouts: 4.33 us -> 1.35 us
where the time goes in v3:
time: 155 us
  Pallas kernels  152 us (98%)
    pallas_call x1, Pallas kernels, window(): pl.pallas_call(functools.partial(window_kernel, n_lon, n_lat), out_shape=...  136 us
    pallas_call x1, Pallas kernels, apply_update(): pl.pallas_call(update_kernel, out_shape=(out, out), in_specs=[vmem, hbm,...  16.2 us

profile of v3, /device:TPU:1, one launch (start us, length us, event | category | flops | bytes accessed | tf_op | source)
XLA Modules:
  0.0 154.7 jit_solution(17820061154986150457)
XLA Ops:
  1.3 1.3 copy.12.courant
  2.6 135.6 %window.1 = (bf16[2048,256]{1,0:T(8,128)(2,1)}, bf16[2048,256]{1,0:T(8,128)(2,1)}, bf16[2048,256]{1,0:T(8,128)(2,1)}, bf16[2048,256]{1,0:T(8,128)(2,1)}, f32[384,128]{1,0:T(8,128)}) custom-call(f32[8,4,64,256]{3,2,1,0:T(8,128)} %prior.1, f32[8,4]{1,0:T(8,128)} %copy.12.courant, f32[1,64]{1,0:T(1,128)} %bitcast.3, f32[16,64,128]{2,1,0:T(8,128)} %geometry.1, ...), custom_call_target="tpu_custom_call" | custom-call | flops 12000000000 | bytes 6000000 | tf_op jit(solution)/shard_map/window/pallas_call | solution.py:353
  138.3 16.2 %update.1 = (f32[2048,256]{1,0:T(8,128)}, f32[2048,256]{1,0:T(8,128)}) custom-call(f32[384,128]{1,0:T(8,128)} %get-tuple-element.9.packed, bf16[2048,256]{1,0:T(8,128)(2,1)} %get-tuple-element.10.prior_high, bf16[2048,256]{1,0:T(8,128)(2,1)} %get-tuple-element.11.prior_low, bf16[2048,256]{1,0:T(8,128)(2,1)} %get-tuple-element.12.end_high, ...), custom_call_target="tpu_custom_call" | custom-call | flops 1700000000 | bytes 8400000 | tf_op jit(solution)/shard_map/update/pallas_call | solution.py:516

commit v4 on v3

v4 whole, which is shorter than its diff:
```python
import functools
import jax
import jax.numpy as jnp
from jax import lax
from jax.experimental import pallas as pl
from jax.experimental.pallas import tpu as pltpu
from jax.sharding import PartitionSpec as P

STEPS = 4
diffusion = 0.08
highest = lax.Precision.HIGHEST
MESH = pl.DeviceIdType.MESH
F32 = jnp.float32
BF16 = jnp.bfloat16

LON, LAT, ALT, WIDE = 8, 4, 64, 256
RAYS, SEG, TILES = 128, 16, 2
ROWS = TILES * RAYS
NEAR = 3 * TILES
PAIRS = LON * LAT // 2
HALF = 128
PACKED = WIDE + HALF
PANEL = 16
CELLS = LON * LAT * ALT
CHUNKS = 8


def split(x):
    high = x.astype(BF16)
    return high, (x - high.astype(F32)).astype(BF16)


def window_kernel(
    n_lon, n_lat,
    prior, courant, survival, geometry, entry_tile, entry_column, entry_segment, entry_counts,
    observed, obs_weight,
    end_out, gram_out,
    s0, s1, s2, s3, s4, s_both, paths, counts, h_high, h_low,
    near, beside, turn_out, turn_in, gram, packed, got_lat, part, got_lon, total, decay, drifts, seen, scales,
    keys, drift_row,
    load_sem, store_sem, swap_send, swap_recv, small_send, small_recv, back_send, back_recv,
    west_send, west_recv, row_send, row_recv, ray_send, ray_recv, turn_send, turn_recv,
    lat_send, lat_recv, lon_send, lon_recv, all_send, all_recv,
):
    lon = lax.axis_index("lon")
    lat = lax.axis_index("lat")
    group = lax.div(lat, 4)
    mine = lax.rem(lax.div(lat, 2), 2)
    core = lax.rem(lat, 2)
    theirs = 1 - mine
    partner = (lon, lat + 2 - 4 * mine)
    states = [s0, s1, s2, s3]

    def at_lon(d):
        return (lax.rem(lon + d + n_lon, n_lon), lat)

    def at_lat(d):
        return (lon, lax.rem(lat + d + n_lat, n_lat))

    def band_of(slot):
        return 4 * group + 2 * slot + core

    def holder(band):
        to = (lon, 4 * lax.div(band, 4) + 2 * mine + lax.rem(band, 2))
        return to, lax.rem(lax.div(band, 2), 2)

    def has_up(slot):
        return band_of(slot) + 1 < n_lat

    def has_down(slot):
        return band_of(slot) > 0

    def remote(src, dst, send, recv, to):
        return pltpu.make_async_remote_copy(
            src_ref=src, dst_ref=dst, send_sem=send, recv_sem=recv, device_id=to, device_id_type=MESH
        )

    def half(index):
        return pl.ds(pl.multiple_of(index * HALF, HALF), HALF)

    cells_of = (slice(1, LON + 1), slice(1, LAT + 1))
    loads = pltpu.make_async_copy(prior.at[:, :, :, half(mine)], s0.at[(mine,) + cells_of], load_sem)
    loads.start()

    slots = entry_tile.shape[2]
    column = entry_column[0]
    live = lax.broadcasted_iota(jnp.int32, (1, slots), 1) < entry_counts[...]
    near_key = (entry_tile[0] - (lat - 1) * TILES) * PAIRS + column // 2
    near_key = jnp.where(live, near_key, -1)
    path_key = entry_segment[0] * 2 + column % 2
    keys[0, 0:1, 0:slots] = near_key
    keys[0, 1:2, 0:slots] = path_key
    drift_row[0] = jnp.broadcast_to(courant[:, 0:1], (LON, HALF))
    lanes = lax.broadcasted_iota(jnp.int32, (LON, HALF), 1)
    for j in range(1, LAT):
        drift_row[0] = jnp.where(lanes == j, jnp.broadcast_to(courant[:, j:j + 1], (LON, HALF)), drift_row[0])

    barrier = pltpu.get_barrier_semaphore()
    for d in range(1, n_lon):
        pl.semaphore_signal(barrier, inc=1, device_id=at_lon(d), device_id_type=MESH)
    for d in range(1, n_lat):
        pl.semaphore_signal(barrier, inc=1, device_id=at_lat(d), device_id_type=MESH)
    pl.semaphore_wait(barrier, n_lon + n_lat - 2)

    def swap():
        return remote(
            prior.at[:, :, :, half(theirs)], s0.at[(mine,) + cells_of], swap_send, swap_recv, partner
        )

    def swapped():
        return remote(
            prior.at[:, :, :, half(theirs)], s0.at[(theirs,) + cells_of], swap_send, swap_recv, partner
        )

    small = [
        remote(keys.at[0], keys.at[1], small_send.at[0], small_recv.at[0], partner),
        remote(drift_row.at[0], drift_row.at[1], small_send.at[1], small_recv.at[1], partner),
    ]
    for copy in small:
        copy.start()
    swap().start()

    def back():
        return remote(
            s4.at[theirs], end_out.at[:, :, :, half(mine)], back_send, back_recv, partner
        )

    def back_landed():
        return remote(
            s4.at[theirs], end_out.at[:, :, :, half(theirs)], back_send, back_recv, partner
        )

    def west_copy(k, s):
        state = states[k]
        return remote(
            state.at[s, LON, 1:LAT + 1], state.at[s, 0, 1:LAT + 1],
            west_send.at[k, s], west_recv.at[k, s], at_lon(1),
        )

    def row_copy(k, s, up):
        to, slot = holder(band_of(s) + (1 if up else -1))
        state = states[k]
        src = state.at[s, 1:LON + 1, LAT if up else 1]
        dst = state.at[slot, 1:LON + 1, 0 if up else LAT + 1]
        return remote(src, dst, row_send.at[k, s, up], row_recv.at[k, slot, up], to)

    def row_landed(k, s, up):
        state = states[k]
        ref = state.at[s, 1:LON + 1, 0 if up else LAT + 1]
        return remote(ref, ref, row_send.at[k, s, up], row_recv.at[k, s, up], partner)

    def ray_copy(k, s, up):
        to, slot = holder(band_of(s) + (1 if up else -1))
        return remote(
            near.at[k, s, 2 if up else 0], beside.at[k, slot, up],
            ray_send.at[k, s, up], ray_recv.at[k, slot, up], to,
        )

    def ray_landed(k, s, up):
        ref = beside.at[k, s, up]
        return remote(ref, ref, ray_send.at[k, s, up], ray_recv.at[k, s, up], partner)

    def turn_copy(k):
        return remote(turn_out.at[k], turn_in.at[k], turn_send.at[k], turn_recv.at[k], partner)

    def out_both(make, k, s, act):
        @pl.when(has_up(s))
        def _():
            act(make(k, s, 1))

        @pl.when(has_down(s))
        def _():
            act(make(k, s, 0))

    def in_both(make, k, s):
        @pl.when(has_down(s))
        def _():
            make(k, s, 1).wait_recv()

        @pl.when(has_up(s))
        def _():
            make(k, s, 0).wait_recv()

    def begin(copy):
        copy.start()

    def sent(copy):
        copy.wait_send()

    def send_edges(k, s):
        out_both(row_copy, k, s, begin)
        west_copy(k, s).start()

    loads.wait()
    send_edges(0, mine)

    for s, up, row, missing in ((0, 1, 0, has_down(0)), (1, 0, LAT + 1, has_up(1))):
        @pl.when(jnp.logical_not(missing))
        def _(s=s, up=up, row=row):
            for k in range(STEPS):
                def clear(i, c, k=k):
                    states[k][s, i + 1, row] = jnp.zeros((ALT, HALF), F32)
                    return c
                lax.fori_loop(0, LON, clear, 0)
                beside[k, s, up] = jnp.zeros((ROWS, HALF), F32)

    def upright(line):
        return jnp.broadcast_to(line, (HALF, HALF)).T

    line = survival[...]
    decay[...] = upright(jnp.concatenate([line, line], axis=1))[0:ALT]
    for k in range(STEPS):
        for t in range(TILES):
            seen[k, t * RAYS:(t + 1) * RAYS] = upright(observed[k, 0, t:t + 1])
            scales[k, t * RAYS:(t + 1) * RAYS] = upright(obs_weight[k, 0, t:t + 1])

    def turn_path(s, c):
        block = geometry[s]
        paths[s] = jnp.concatenate([block, block], axis=0).T
        return c

    lax.fori_loop(0, SEG, turn_path, 0)

    for copy in small:
        copy.wait_recv()
    wide_half = lax.broadcasted_iota(jnp.int32, (HALF, slots), 0) // ALT
    for slot in range(2):
        own = mine == slot
        at_key = jnp.where(own, keys[0, 0:1, 0:slots], keys[1, 0:1, 0:slots])
        by_path = jnp.where(own, keys[0, 1:2, 0:slots], keys[1, 1:2, 0:slots])
        left = (lax.broadcasted_iota(jnp.int32, (NEAR * PAIRS, slots), 0) == at_key).astype(F32).astype(BF16)
        for s in range(SEG):
            right = (wide_half + 2 * s == by_path).astype(F32).astype(BF16)
            counts[slot * NEAR * PAIRS:(slot + 1) * NEAR * PAIRS, s] = lax.dot_general(
                left, right, (((1,), (1,)), ((), ())), preferred_element_type=F32
            )
        drift_of = jnp.where(own, drift_row[0], drift_row[1])
        for j in range(LAT):
            across_lanes = jnp.broadcast_to(drift_of[:, j:j + 1], (LON, HALF))
            for i in range(LON):
                drifts[slot, i, j] = jnp.broadcast_to(across_lanes[i:i + 1], (8, HALF))

    def build_tile(t, c):
        def build(p, c2):
            number = counts[t * PAIRS + p]
            total_path = number[0:1] * paths[0]
            for s in range(1, SEG):
                total_path += number[s:s + 1] * paths[s]
            high, low = split(total_path)
            at = (pl.ds(pl.multiple_of(t * RAYS, RAYS), RAYS), half(p))
            h_high[at] = high
            h_low[at] = low
            return c2

        return lax.fori_loop(0, PAIRS, build, c)

    lax.fori_loop(0, 2 * NEAR, build_tile, 0)
    gram[...] = jnp.zeros((WIDE, WIDE), F32)

    def cell(k, s, i, j):
        old = states[k]
        drift = drifts[s, i, j, 0:1]
        keep = 1.0 - 2.0 * diffusion - drift
        new = keep * old[s, i + 1, j + 1] + drift * old[s, i, j + 1]
        new += diffusion * (old[s, i + 1, j + 2] + old[s, i + 1, j])
        new = new * decay[...]
        if k + 1 < STEPS:
            states[k + 1][s, i + 1, j + 1] = new
        else:
            s4[s, i, j] = new
        at = pl.ds(pl.multiple_of(((s * LON + i) * LAT + j) * ALT, ALT), ALT)
        high, low = split(new)
        s_both[at, 0:HALF] = high
        s_both[at, HALF:WIDE] = low

    def cells(k, first, last, rows):
        def one(n, c):
            s = lax.div(n, last - first)
            i = first + lax.rem(n, last - first)
            for j in rows:
                cell(k, s, i, j)
            return c

        lax.fori_loop(0, 2 * (last - first), one, 0)

    def project(k):
        for s in range(2):
            def part_of(b, c, s=s):
                at = pl.ds(pl.multiple_of(b * 256, 256), 256)
                both = s_both[pl.ds(pl.multiple_of(s * CELLS + b * 256, 256), 256)]
                rays = slice(s * NEAR * RAYS, (s + 1) * NEAR * RAYS)
                add = jnp.dot(h_high[rays, at], both, preferred_element_type=F32)
                add = add[:, 0:HALF] + add[:, HALF:WIDE]
                add += jnp.dot(h_low[rays, at], both[:, 0:HALF], preferred_element_type=F32)
                add = add.reshape(3, ROWS, HALF)

                @pl.when(b == 0)
                def _():
                    near[k, s] = add

                @pl.when(b > 0)
                def _():
                    near[k, s] += add

                return c

            lax.fori_loop(0, CELLS // 256, part_of, 0)
            out_both(ray_copy, k, s, begin)

    def turn(k):
        in_both(ray_landed, k, theirs)
        turn_out[k] = near[k, theirs, 1] + beside[k, theirs, 0] + beside[k, theirs, 1]
        turn_copy(k).start()

    def add_gram(k):
        in_both(ray_landed, k, mine)
        here = near[k, mine, 1] + beside[k, mine, 0] + beside[k, mine, 1]
        turn_copy(k).wait_recv()
        there = turn_in[k]
        first = mine == 0
        low = jnp.where(first, here, there)
        high = jnp.where(first, there, here)
        lane = lax.broadcasted_iota(jnp.int32, (ROWS, HALF), 1)
        low = jnp.where(lane == 0, seen[k] - low, low) * scales[k]
        high = high * scales[k]
        rays = jnp.concatenate([low, high], axis=1)
        gram[...] += jnp.dot(rays.T, rays, precision=highest, preferred_element_type=F32)

    swapped().wait_recv()
    send_edges(0, theirs)
    for k in range(STEPS):
        cells(k, 1, LON, range(1, LAT - 1))
        for s in range(2):
            west_copy(k, s).wait_recv()
        cells(k, 0, 1, range(1, LAT - 1))
        for s in range(2):
            in_both(row_landed, k, s)
        cells(k, 0, LON, (0, LAT - 1))
        if k + 1 < STEPS:
            for s in range(2):
                send_edges(k + 1, s)
        else:
            store = pltpu.make_async_copy(s4.at[mine], end_out.at[:, :, :, half(mine)], store_sem)
            store.start()
            back().start()
        if k > 0:
            turn(k - 1)
        project(k)
        if k > 1:
            add_gram(k - 2)
    add_gram(STEPS - 2)
    turn(STEPS - 1)
    add_gram(STEPS - 1)

    packed[0:WIDE] = gram[:, 0:HALF]
    packed[WIDE:PACKED] = gram[HALF:WIDE, HALF:WIDE]
    piece = PACKED // n_lat

    def own(index):
        return pl.ds(pl.multiple_of(index * piece, 8), piece)

    def scatter(d):
        to = lax.rem(lat + d, n_lat)
        return remote(packed.at[own(to)], got_lat.at[d], lat_send.at[d], lat_recv.at[d], at_lat(d))

    def across(d):
        return remote(part, got_lon.at[d], lon_send.at[d], lon_recv.at[d], at_lon(d))

    def gather(d):
        return remote(total.at[own(lat)], total.at[own(lat)], all_send.at[d], all_recv.at[d], at_lat(d))

    def landed(d):
        from_lat = lax.rem(lat - d + n_lat, n_lat)
        return remote(total.at[own(from_lat)], total.at[own(from_lat)], all_send.at[d], all_recv.at[d], at_lat(d))

    for d in range(1, n_lat):
        scatter(d).start()
    acc = packed[own(lat)]
    for d in range(1, n_lat):
        scatter(d).wait_recv()
        acc += got_lat[d]
    part[...] = acc
    for d in range(1, n_lon):
        across(d).start()
    for d in range(1, n_lon):
        across(d).wait_recv()
        acc += got_lon[d]
    total[own(lat)] = acc
    for d in range(1, n_lat):
        gather(d).start()
    for d in range(1, n_lat):
        landed(d).wait_recv()
    gram_out[...] = total[...]

    back_landed().wait_recv()
    store.wait()
    back().wait_send()
    swap().wait_send()
    for copy in small:
        copy.wait_send()
    for k in range(STEPS):
        turn_copy(k).wait_send()
        for s in range(2):
            west_copy(k, s).wait_send()
            out_both(row_copy, k, s, sent)
            out_both(ray_copy, k, s, sent)
    for d in range(1, n_lat):
        scatter(d).wait_send()
        gather(d).wait_send()
    for d in range(1, n_lon):
        across(d).wait_send()


def window(n_lon, n_lat, *operands):
    piece = PACKED // n_lat
    ghosts = pltpu.VMEM((2, LON + 1, LAT + 2, ALT, HALF), F32)
    vmem = pl.BlockSpec(memory_space=pltpu.VMEM)
    hbm = pl.BlockSpec(memory_space=pl.ANY)
    dma = pltpu.SemaphoreType.DMA
    return pl.pallas_call(
        functools.partial(window_kernel, n_lon, n_lat),
        out_shape=(
            jax.ShapeDtypeStruct((LON, LAT, ALT, WIDE), F32),
            jax.ShapeDtypeStruct((PACKED, HALF), F32),
        ),
        in_specs=[hbm] + [vmem] * 9,
        out_specs=(hbm, vmem),
        scratch_shapes=[
            ghosts, ghosts, ghosts, ghosts,
            pltpu.VMEM((2, LON, LAT, ALT, HALF), F32),
            pltpu.VMEM((2 * CELLS, WIDE), BF16),
            pltpu.VMEM((SEG, RAYS, HALF), F32),
            pltpu.VMEM((2 * NEAR * PAIRS, SEG, HALF), F32),
            pltpu.VMEM((2 * NEAR * RAYS, CELLS), BF16),
            pltpu.VMEM((2 * NEAR * RAYS, CELLS), BF16),
            pltpu.VMEM((STEPS, 2, 3, ROWS, HALF), F32),
            pltpu.VMEM((STEPS, 2, 2, ROWS, HALF), F32),
            pltpu.VMEM((STEPS, ROWS, HALF), F32),
            pltpu.VMEM((STEPS, ROWS, HALF), F32),
            pltpu.VMEM((WIDE, WIDE), F32),
            pltpu.VMEM((PACKED, HALF), F32),
            pltpu.VMEM((n_lat, piece, HALF), F32),
            pltpu.VMEM((piece, HALF), F32),
            pltpu.VMEM((n_lon, piece, HALF), F32),
            pltpu.VMEM((PACKED, HALF), F32),
            pltpu.VMEM((ALT, HALF), F32),
            pltpu.VMEM((2, LON, LAT, 8, HALF), F32),
            pltpu.VMEM((STEPS, ROWS, HALF), F32),
            pltpu.VMEM((STEPS, ROWS, HALF), F32),
            pltpu.VMEM((2, 8, HALF), jnp.int32),
            pltpu.VMEM((2, LON, HALF), F32),
            dma, dma, dma, dma, dma((2,)), dma((2,)), dma, dma,
            dma((STEPS, 2)), dma((STEPS, 2)),
            dma((STEPS, 2, 2)), dma((STEPS, 2, 2)),
            dma((STEPS, 2, 2)), dma((STEPS, 2, 2)),
            dma((STEPS,)), dma((STEPS,)),
            dma((n_lat,)), dma((n_lat,)),
            dma((n_lon,)), dma((n_lon,)),
            dma((n_lat,)), dma((n_lat,)),
        ],
        compiler_params=pltpu.CompilerParams(
            collective_id=0, has_side_effects=True, vmem_limit_bytes=60 * 1024 * 1024
        ),
        cost_estimate=pl.CostEstimate(flops=12_000_000_000, bytes_accessed=6_000_000, transcendentals=0),
        name="window",
    )(*operands)


def panel_rows(block, at, rows_low, rows_high):
    spread = {}
    for j in range(PANEL):
        column = jnp.broadcast_to(block[:, at + j:at + j + 1], (PANEL, HALF))
        for i in range(j, PANEL):
            spread[i, j] = jnp.broadcast_to(column[i:i + 1], (8, HALF))
    rows = [
        [jnp.broadcast_to(part[i:i + 1], (8, HALF)) for part in (rows_low, rows_high)]
        for i in range(PANEL)
    ]
    for k in range(PANEL):
        scale = lax.rsqrt(spread[k, k])
        for i in range(k + 1, PANEL):
            spread[i, k] = spread[i, k] * scale
        rows[k] = [part * scale for part in rows[k]]
        for i in range(k + 1, PANEL):
            factor = spread[i, k]
            for j in range(k + 1, i + 1):
                spread[i, j] = spread[i, j] - factor * spread[j, k]
            rows[i] = [a - factor * b for a, b in zip(rows[i], rows[k])]
    return rows


def update_kernel(packed, prior, end, start_out, end_out,
                  work, inverse, panel, u_high, u_low, z, results, load_sem, store_sem):
    sources = (prior, end)
    loads = [pltpu.make_async_copy(src, z.at[n], load_sem.at[n]) for n, src in enumerate(sources)]
    for copy in loads:
        copy.start()

    lower = packed[0:WIDE]
    corner = lower[HALF:WIDE].T
    row = lax.broadcasted_iota(jnp.int32, (HALF, HALF), 0)
    lane = lax.broadcasted_iota(jnp.int32, (HALF, HALF), 1)
    same = (row == lane).astype(F32)
    inner = jnp.logical_and(row > 0, lane > 0)
    work[0:HALF, 0:HALF] = jnp.where(inner, lower[0:HALF], 0.0) + same
    work[0:HALF, HALF:WIDE] = jnp.where(row > 0, corner, 0.0)
    work[HALF:WIDE, 0:HALF] = jnp.where(lane > 0, lower[HALF:WIDE], 0.0)
    work[HALF:WIDE, HALF:WIDE] = packed[WIDE:PACKED] + same

    for p in range(WIDE // PANEL):
        first = p * PANEL
        side, at = first // HALF, first % HALF
        mine = slice(first, first + PANEL)
        lanes = lax.broadcasted_iota(jnp.int32, (PANEL, HALF), 1)
        rows_of = lax.broadcasted_iota(jnp.int32, (PANEL, HALF), 0)
        parts = [work[mine, 0:HALF], work[mine, HALF:WIDE]]
        block = parts[side]
        in_panel = jnp.logical_and(lanes >= at, lanes < at + PANEL)
        unit = (lanes == rows_of + at).astype(F32)
        if p == 0:
            right = jnp.logical_and(lanes == 0, rows_of > 0)
            unit = jnp.where(right, lower[mine], unit)
        parts[side] = jnp.where(in_panel, unit, block)
        rows = panel_rows(block, at, *parts)
        for i in range(PANEL):
            for h in range(2):
                panel[i:i + 1, h * HALF:(h + 1) * HALF] = rows[i][h][0:1]
        done = panel[...]
        wide = lax.broadcasted_iota(jnp.int32, (PANEL, WIDE), 1)
        inverse[mine] = jnp.where(wide < first + PANEL, done, 0.0)
        rest = first + PANEL
        if rest == WIDE:
            break
        high, low = split(done)
        left = jnp.concatenate([high, high, low], axis=0)
        both = jnp.concatenate([high, low, high], axis=0)
        begin = HALF if rest >= HALF else 0
        change = lax.dot_general(
            left[:, begin:], both, (((0,), (0,)), ((), ())), preferred_element_type=F32
        )
        old = work[rest:WIDE]
        wide = lax.broadcasted_iota(jnp.int32, (WIDE - rest, WIDE), 1)
        blank = jnp.logical_and(wide >= first, wide < rest)
        if p == 0:
            start = jnp.where(lane[0:1] == 0, lower[rest:WIDE], 0.0)
            start = jnp.concatenate([start, jnp.zeros_like(start)], axis=1)
            old = jnp.where(blank, start, old)
        else:
            old = jnp.where(blank, 0.0, old)
        work[rest:WIDE] = old - change[rest - begin:]

    whole = inverse[...]
    wide = lax.broadcasted_iota(jnp.int32, (WIDE, WIDE), 1)
    tall = lax.broadcasted_iota(jnp.int32, (WIDE, WIDE), 0)
    right = jnp.where(tall[:, 0:1] > 0, whole[:, 0:1], 0.0)
    whole = jnp.where(jnp.logical_and(wide == 0, tall > 0), 0.0, whole)
    weights = jnp.sum(right * whole, axis=0, keepdims=True)
    turned = jnp.where(tall == 0, whole + weights, whole)
    high, low = split(turned.T)
    u_high[...] = high
    u_low[...] = low

    for copy in loads:
        copy.wait()
    size = CELLS // CHUNKS
    stores = []
    for n, out in enumerate((start_out, end_out)):
        for b in range(CHUNKS):
            at = slice(b * size, (b + 1) * size)
            a_high, a_low = split(z[n, at])
            value = jnp.dot(a_high, u_high[...], preferred_element_type=F32)
            value += jnp.dot(a_low, u_high[...], preferred_element_type=F32)
            value += jnp.dot(a_high, u_low[...], preferred_element_type=F32)
            results[n, at] = value
            copy = pltpu.make_async_copy(results.at[n, at], out.at[at], store_sem.at[n, b])
            copy.start()
            stores.append(copy)
    for copy in stores:
        copy.wait()


def apply_update(packed, prior, end):
    vmem = pl.BlockSpec(memory_space=pltpu.VMEM)
    hbm = pl.BlockSpec(memory_space=pl.ANY)
    out = jax.ShapeDtypeStruct((CELLS, WIDE), F32)
    return pl.pallas_call(
        update_kernel,
        out_shape=(out, out),
        in_specs=[vmem, hbm, hbm],
        out_specs=(hbm, hbm),
        scratch_shapes=[
            pltpu.VMEM((WIDE, WIDE), F32),
            pltpu.VMEM((WIDE, WIDE), F32),
            pltpu.VMEM((PANEL, WIDE), F32),
            pltpu.VMEM((WIDE, WIDE), BF16),
            pltpu.VMEM((WIDE, WIDE), BF16),
            pltpu.VMEM((2, CELLS, WIDE), F32),
            pltpu.VMEM((2, CELLS, WIDE), F32),
            pltpu.SemaphoreType.DMA((2,)),
            pltpu.SemaphoreType.DMA((2, CHUNKS)),
        ],
        compiler_params=pltpu.CompilerParams(vmem_limit_bytes=60 * 1024 * 1024),
        cost_estimate=pl.CostEstimate(flops=1_700_000_000, bytes_accessed=8_400_000, transcendentals=0),
        name="update",
    )(packed, prior, end)


def shards(
    prior_state,
    courant,
    cell_survival_rate,
    geometry,
    entry_tile,
    entry_column,
    entry_segment,
    entry_counts,
    observed,
    obs_weight,
):
    n_lon, n_lat = lax.axis_size("lon"), lax.axis_size("lat")
    forecast, packed = window(
        n_lon, n_lat,
        prior_state, courant, cell_survival_rate[None, :], geometry,
        entry_tile, entry_column, entry_segment, entry_counts, observed, obs_weight,
    )
    start_state, end_state = apply_update(
        packed, prior_state.reshape(CELLS, WIDE), forecast.reshape(CELLS, WIDE)
    )
    return (start_state.reshape(prior_state.shape), end_state.reshape(prior_state.shape))


def solution(mesh):
    placed = (
        P("lon", "lat", None, None),
        P("lon", "lat"),
        P(),
        P(),
        P("lon", "lat", None),
        P("lon", "lat", None),
        P("lon", "lat", None),
        P("lon", "lat"),
        P(None, "lon", "lat", None),
        P(None, "lon", "lat", None),
    )
    return jax.shard_map(
        shards,
        mesh=mesh,
        in_specs=placed,
        out_specs=(P("lon", "lat", None, None), P("lon", "lat", None, None)),
        check_vma=False,
    )
```

time: 155 us -> 141 us (0.910)
  Pallas kernels: 152 us -> 138 us
    pallas_call x1, Pallas kernels: 136 us -> 122 us  [window(): pl.pallas_call(functools.partial(window_kernel, n_lon, n_lat), out_shape=...]
where the time goes in v4:
time: 141 us
  Pallas kernels  138 us (98%)
  between operations  1.45 us (1%)
    pallas_call x1, Pallas kernels, window(): pl.pallas_call(functools.partial(window_kernel, n_lon, n_lat), out_shape=...  122 us
    pallas_call x1, Pallas kernels, apply_update(): pl.pallas_call(update_kernel, out_shape=(out, out), in_specs=[vmem, hbm,...  16.4 us

profile of v4, /device:TPU:1, one launch (start us, length us, event | category | flops | bytes accessed | tf_op | source)
XLA Modules:
  0.0 140.9 jit_solution(777202508790654531)
XLA Ops:
  1.3 1.3 copy.12.courant
  2.6 121.7 %window.1 = (f32[8,4,64,256]{3,2,1,0:T(8,128)}, f32[384,128]{1,0:T(8,128)}) custom-call(f32[8,4,64,256]{3,2,1,0:T(8,128)} %prior.1, f32[8,4]{1,0:T(8,128)} %copy.12.courant, f32[1,64]{1,0:T(1,128)} %bitcast.6, f32[16,64,128]{2,1,0:T(8,128)} %geometry.1, s32[1,1,64]{2,1,0:T(1,128)} %entry_tile.1, s32[1,1,64]{2,1,0:T(1,128)} %entry_column.1, ...), custom_call_target="tpu_custom_call" | custom-call | flops 12000000000 | bytes 6000000 | tf_op jit(solution)/shard_map/window/pallas_call | solution.py:420
  124.4 16.4 %update.1 = (f32[2048,256]{1,0:T(8,128)}, f32[2048,256]{1,0:T(8,128)}) custom-call(f32[384,128]{1,0:T(8,128)} %get-tuple-element.6.packed, f32[2048,256]{1,0:T(8,128)} %bitcast.5, f32[2048,256]{1,0:T(8,128)} %bitcast.9), custom_call_target="tpu_custom_call" | custom-call | flops 1700000000 | bytes 8400000 | tf_op jit(solution)/shard_map/update/pallas_call | solution.py:586

commit v5 on v4

--- a/solution.py
+++ b/solution.py
@@ -22,7 +22,8 @@
 PACKED = WIDE + HALF
 PANEL = 16
 CELLS = LON * LAT * ALT
-CHUNKS = 8
+CHUNKS = 4
+EARLY = 2
 
 
 def split(x):
@@ -34,10 +35,10 @@
     n_lon, n_lat,
     prior, courant, survival, geometry, entry_tile, entry_column, entry_segment, entry_counts,
     observed, obs_weight,
-    end_out, gram_out,
+    end_out, u_high, u_low,
     s0, s1, s2, s3, s4, s_both, paths, counts, h_high, h_low,
     near, beside, turn_out, turn_in, gram, packed, got_lat, part, got_lon, total, decay, drifts, seen, scales,
-    keys, drift_row,
+    keys, drift_row, work, inverse, panel,
     load_sem, store_sem, swap_send, swap_recv, small_send, small_recv, back_send, back_recv,
     west_send, west_recv, row_send, row_recv, ray_send, ray_recv, turn_send, turn_recv,
     lat_send, lat_recv, lon_send, lon_recv, all_send, all_recv,
@@ -120,14 +121,14 @@
         copy.start()
     swap().start()
 
-    def back():
+    def back(i):
         return remote(
-            s4.at[theirs], end_out.at[:, :, :, half(mine)], back_send, back_recv, partner
-        )
-
-    def back_landed():
+            s4.at[theirs, i], end_out.at[i, :, :, half(mine)], back_send.at[i], back_recv.at[i], partner
+        )
+
+    def back_landed(i):
         return remote(
-            s4.at[theirs], end_out.at[:, :, :, half(theirs)], back_send, back_recv, partner
+            s4.at[theirs, i], end_out.at[i, :, :, half(theirs)], back_send.at[i], back_recv.at[i], partner
         )
 
     def west_copy(k, s):
@@ -342,7 +343,8 @@
         else:
             store = pltpu.make_async_copy(s4.at[mine], end_out.at[:, :, :, half(mine)], store_sem)
             store.start()
-            back().start()
+            for i in range(EARLY):
+                back(i).start()
         if k > 0:
             turn(k - 1)
         project(k)
@@ -390,11 +392,14 @@
         gather(d).start()
     for d in range(1, n_lat):
         landed(d).wait_recv()
-    gram_out[...] = total[...]
-
-    back_landed().wait_recv()
+    for i in range(EARLY, LON):
+        back(i).start()
+    u_high[...], u_low[...] = update_matrix(total, work, inverse, panel)
+
     store.wait()
-    back().wait_send()
+    for i in range(LON):
+        back_landed(i).wait_recv()
+        back(i).wait_send()
     swap().wait_send()
     for copy in small:
         copy.wait_send()
@@ -421,10 +426,11 @@
         functools.partial(window_kernel, n_lon, n_lat),
         out_shape=(
             jax.ShapeDtypeStruct((LON, LAT, ALT, WIDE), F32),
-            jax.ShapeDtypeStruct((PACKED, HALF), F32),
+            jax.ShapeDtypeStruct((WIDE, WIDE), BF16),
+            jax.ShapeDtypeStruct((WIDE, WIDE), BF16),
         ),
         in_specs=[hbm] + [vmem] * 9,
-        out_specs=(hbm, vmem),
+        out_specs=(hbm, vmem, vmem),
         scratch_shapes=[
             ghosts, ghosts, ghosts, ghosts,
             pltpu.VMEM((2, LON, LAT, ALT, HALF), F32),
@@ -449,7 +455,10 @@
             pltpu.VMEM((STEPS, ROWS, HALF), F32),
             pltpu.VMEM((2, 8, HALF), jnp.int32),
             pltpu.VMEM((2, LON, HALF), F32),
-            dma, dma, dma, dma, dma((2,)), dma((2,)), dma, dma,
+            pltpu.VMEM((WIDE, WIDE), F32),
+            pltpu.VMEM((WIDE, WIDE), F32),
+            pltpu.VMEM((PANEL, WIDE), F32),
+            dma, dma, dma, dma, dma((2,)), dma((2,)), dma((LON,)), dma((LON,)),
             dma((STEPS, 2)), dma((STEPS, 2)),
             dma((STEPS, 2, 2)), dma((STEPS, 2, 2)),
             dma((STEPS, 2, 2)), dma((STEPS, 2, 2)),
@@ -466,36 +475,30 @@
     )(*operands)
 
 
-def panel_rows(block, at, rows_low, rows_high):
-    spread = {}
-    for j in range(PANEL):
-        column = jnp.broadcast_to(block[:, at + j:at + j + 1], (PANEL, HALF))
-        for i in range(j, PANEL):
-            spread[i, j] = jnp.broadcast_to(column[i:i + 1], (8, HALF))
-    rows = [
-        [jnp.broadcast_to(part[i:i + 1], (8, HALF)) for part in (rows_low, rows_high)]
-        for i in range(PANEL)
+def panel_rows(block, at, *parts):
+    def spread(x):
+        return jnp.broadcast_to(x[:, None, :], (x.shape[0], 8, HALF))
+
+    columns = [
+        spread(jnp.broadcast_to(block[:, at + j:at + j + 1], (PANEL, HALF))[j:]) for j in range(PANEL)
     ]
+    parts = [spread(part) for part in parts]
+    done = [[] for _ in parts]
     for k in range(PANEL):
-        scale = lax.rsqrt(spread[k, k])
-        for i in range(k + 1, PANEL):
-            spread[i, k] = spread[i, k] * scale
-        rows[k] = [part * scale for part in rows[k]]
-        for i in range(k + 1, PANEL):
-            factor = spread[i, k]
-            for j in range(k + 1, i + 1):
-                spread[i, j] = spread[i, j] - factor * spread[j, k]
-            rows[i] = [a - factor * b for a, b in zip(rows[i], rows[k])]
-    return rows
-
-
-def update_kernel(packed, prior, end, start_out, end_out,
-                  work, inverse, panel, u_high, u_low, z, results, load_sem, store_sem):
-    sources = (prior, end)
-    loads = [pltpu.make_async_copy(src, z.at[n], load_sem.at[n]) for n, src in enumerate(sources)]
-    for copy in loads:
-        copy.start()
-
+        scale = lax.rsqrt(columns[k][0:1])
+        factor = columns[k][1:] * scale
+        for n, part in enumerate(parts):
+            top = part[0:1] * scale
+            done[n].append(top)
+            if k + 1 < PANEL:
+                parts[n] = part[1:] - factor * top
+        for j in range(k + 1, PANEL):
+            rest = factor[j - k - 1:]
+            columns[j] = columns[j] - rest * rest[0:1]
+    return done
+
+
+def update_matrix(packed, work, inverse, panel):
     lower = packed[0:WIDE]
     corner = lower[HALF:WIDE].T
     row = lax.broadcasted_iota(jnp.int32, (HALF, HALF), 0)
@@ -521,10 +524,9 @@
             right = jnp.logical_and(lanes == 0, rows_of > 0)
             unit = jnp.where(right, lower[mine], unit)
         parts[side] = jnp.where(in_panel, unit, block)
-        rows = panel_rows(block, at, *parts)
-        for i in range(PANEL):
-            for h in range(2):
-                panel[i:i + 1, h * HALF:(h + 1) * HALF] = rows[i][h][0:1]
+        for h, done in enumerate(panel_rows(block, at, *parts)):
+            for i in range(PANEL):
+                panel[i:i + 1, h * HALF:(h + 1) * HALF] = done[i][0, 0:1]
         done = panel[...]
         wide = lax.broadcasted_iota(jnp.int32, (PANEL, WIDE), 1)
         inverse[mine] = jnp.where(wide < first + PANEL, done, 0.0)
@@ -556,53 +558,52 @@
     whole = jnp.where(jnp.logical_and(wide == 0, tall > 0), 0.0, whole)
     weights = jnp.sum(right * whole, axis=0, keepdims=True)
     turned = jnp.where(tall == 0, whole + weights, whole)
-    high, low = split(turned.T)
-    u_high[...] = high
-    u_low[...] = low
-
+    return split(turned.T)
+
+
+def apply_kernel(u_high, u_low, prior, end, start_out, end_out, z, results, load_sem, store_sem):
+    size = CELLS // CHUNKS
+    pieces = [(n, b, slice(b * size, (b + 1) * size)) for n in range(2) for b in range(CHUNKS)]
+    loads = [
+        pltpu.make_async_copy((prior, end)[n].at[at], z.at[n, at], load_sem.at[n, b]) for n, b, at in pieces
+    ]
+    stores = [
+        pltpu.make_async_copy(results.at[n, at], (start_out, end_out)[n].at[at], store_sem.at[n, b])
+        for n, b, at in pieces
+    ]
     for copy in loads:
-        copy.wait()
-    size = CELLS // CHUNKS
-    stores = []
-    for n, out in enumerate((start_out, end_out)):
-        for b in range(CHUNKS):
-            at = slice(b * size, (b + 1) * size)
-            a_high, a_low = split(z[n, at])
-            value = jnp.dot(a_high, u_high[...], preferred_element_type=F32)
-            value += jnp.dot(a_low, u_high[...], preferred_element_type=F32)
-            value += jnp.dot(a_high, u_low[...], preferred_element_type=F32)
-            results[n, at] = value
-            copy = pltpu.make_async_copy(results.at[n, at], out.at[at], store_sem.at[n, b])
-            copy.start()
-            stores.append(copy)
+        copy.start()
+    for (n, b, at), load, store in zip(pieces, loads, stores):
+        load.wait()
+        a_high, a_low = split(z[n, at])
+        value = jnp.dot(jnp.concatenate([a_high, a_low], axis=0), u_high[...], preferred_element_type=F32)
+        value = value[:size] + value[size:]
+        value += jnp.dot(a_high, u_low[...], preferred_element_type=F32)
+        results[n, at] = value
+        store.start()
     for copy in stores:
         copy.wait()
 
 
-def apply_update(packed, prior, end):
+def apply_update(u_high, u_low, prior, end):
     vmem = pl.BlockSpec(memory_space=pltpu.VMEM)
     hbm = pl.BlockSpec(memory_space=pl.ANY)
     out = jax.ShapeDtypeStruct((CELLS, WIDE), F32)
     return pl.pallas_call(
-        update_kernel,
+        apply_kernel,
         out_shape=(out, out),
-        in_specs=[vmem, hbm, hbm],
+        in_specs=[vmem, vmem, hbm, hbm],
         out_specs=(hbm, hbm),
         scratch_shapes=[
-            pltpu.VMEM((WIDE, WIDE), F32),
-            pltpu.VMEM((WIDE, WIDE), F32),
-            pltpu.VMEM((PANEL, WIDE), F32),
-            pltpu.VMEM((WIDE, WIDE), BF16),
-            pltpu.VMEM((WIDE, WIDE), BF16),
             pltpu.VMEM((2, CELLS, WIDE), F32),
             pltpu.VMEM((2, CELLS, WIDE), F32),
-            pltpu.SemaphoreType.DMA((2,)),
+            pltpu.SemaphoreType.DMA((2, CHUNKS)),
             pltpu.SemaphoreType.DMA((2, CHUNKS)),
         ],
         compiler_params=pltpu.CompilerParams(vmem_limit_bytes=60 * 1024 * 1024),
         cost_estimate=pl.CostEstimate(flops=1_700_000_000, bytes_accessed=8_400_000, transcendentals=0),
         name="update",
-    )(packed, prior, end)
+    )(u_high, u_low, prior, end)
 
 
 def shards(
@@ -618,13 +619,13 @@
     obs_weight,
 ):
     n_lon, n_lat = lax.axis_size("lon"), lax.axis_size("lat")
-    forecast, packed = window(
+    forecast, u_high, u_low = window(
         n_lon, n_lat,
         prior_state, courant, cell_survival_rate[None, :], geometry,
         entry_tile, entry_column, entry_segment, entry_counts, observed, obs_weight,
     )
     start_state, end_state = apply_update(
-        packed, prior_state.reshape(CELLS, WIDE), forecast.reshape(CELLS, WIDE)
+        u_high, u_low, prior_state.reshape(CELLS, WIDE), forecast.reshape(CELLS, WIDE)
     )
     return (start_state.reshape(prior_state.shape), end_state.reshape(prior_state.shape))
 

time: 141 us -> 134 us (0.950)
  Pallas kernels: 138 us -> 131 us
    pallas_call x1, Pallas kernels: 16.4 us -> 7.39 us  [apply_update(): pl.pallas_call(apply_kernel, out_shape=(out, out), in_specs=[vmem, vmem,...]
    pallas_call x1, Pallas kernels: 122 us -> 123 us  [window(): pl.pallas_call(functools.partial(window_kernel, n_lon, n_lat), out_shape=...]
where the time goes in v5:
time: 134 us
  Pallas kernels  131 us (98%)
  between operations  1.45 us (1%)
  local copies, waits for them, and re-layouts  1.35 us (1%)
    pallas_call x1, Pallas kernels, window(): pl.pallas_call(functools.partial(window_kernel, n_lon, n_lat), out_shape=...  123 us
    pallas_call x1, Pallas kernels, apply_update(): pl.pallas_call(apply_kernel, out_shape=(out, out), in_specs=[vmem, vmem,...  7.39 us

profile of v5, /device:TPU:1, one launch (start us, length us, event | category | flops | bytes accessed | tf_op | source)
XLA Modules:
  0.0 133.5 jit_solution(6828615516055577982)
XLA Ops:
  1.3 1.3 %copy.12.courant = f32[8,4]{1,0:T(8,128)} copy(f32[8,4]{0,1:T(4,128)} %param.11) | data formatting | bytes 256 | tf_op args[1]
  2.6 123.4 %window.1 = (f32[8,4,64,256]{3,2,1,0:T(8,128)}, bf16[256,256]{1,0:T(8,128)(2,1)}, bf16[256,256]{1,0:T(8,128)(2,1)}) custom-call(f32[8,4,64,256]{3,2,1,0:T(8,128)} %prior.1, f32[8,4]{1,0:T(8,128)} %copy.12.courant, f32[1,64]{1,0:T(1,128)} %bitcast.6, f32[16,64,128]{2,1,0:T(8,128)} %geometry.1, s32[1,1,64]{2,1,0:T(1,128)} %entry_tile.1, ...), custom_call_target="tpu_custom_call" | custom-call | flops 12000000000 | bytes 6000000 | tf_op jit(solution)/shard_map/window/pallas_call | solution.py:425
  126.0 7.4 %update.1 = (f32[2048,256]{1,0:T(8,128)}, f32[2048,256]{1,0:T(8,128)}) custom-call(bf16[256,256]{1,0:T(8,128)(2,1)} %get-tuple-element.7.u_high, bf16[256,256]{1,0:T(8,128)(2,1)} %get-tuple-element.8.u_low, f32[2048,256]{1,0:T(8,128)} %bitcast.5, f32[2048,256]{1,0:T(8,128)} %bitcast.9), custom_call_target="tpu_custom_call" | custom-call | flops 1700000000 | bytes 8400000 | tf_op jit(solution)/shard_map/update/pallas_call | solution.py:592

commit v6 on v5

--- a/solution.py
+++ b/solution.py
@@ -24,6 +24,9 @@
 CELLS = LON * LAT * ALT
 CHUNKS = 4
 EARLY = 2
+BESIDE_SCATTER = 3
+BESIDE_ACROSS = 4
+BESIDE_GATHER = 6
 
 
 def split(x):
@@ -91,10 +94,7 @@
     path_key = entry_segment[0] * 2 + column % 2
     keys[0, 0:1, 0:slots] = near_key
     keys[0, 1:2, 0:slots] = path_key
-    drift_row[0] = jnp.broadcast_to(courant[:, 0:1], (LON, HALF))
-    lanes = lax.broadcasted_iota(jnp.int32, (LON, HALF), 1)
-    for j in range(1, LAT):
-        drift_row[0] = jnp.where(lanes == j, jnp.broadcast_to(courant[:, j:j + 1], (LON, HALF)), drift_row[0])
+    drift_row[0, 0:LAT, 0:LON] = courant[...]
 
     barrier = pltpu.get_barrier_semaphore()
     for d in range(1, n_lon):
@@ -236,10 +236,10 @@
                 left, right, (((1,), (1,)), ((), ())), preferred_element_type=F32
             )
         drift_of = jnp.where(own, drift_row[0], drift_row[1])
-        for j in range(LAT):
-            across_lanes = jnp.broadcast_to(drift_of[:, j:j + 1], (LON, HALF))
-            for i in range(LON):
-                drifts[slot, i, j] = jnp.broadcast_to(across_lanes[i:i + 1], (8, HALF))
+        for i in range(LON):
+            across_lanes = jnp.broadcast_to(drift_of[:, i:i + 1], (8, HALF))
+            for j in range(LAT):
+                drifts[slot, i, j] = jnp.broadcast_to(across_lanes[j:j + 1], (8, HALF))
 
     def build_tile(t, c):
         def build(p, c2):
@@ -269,43 +269,34 @@
             states[k + 1][s, i + 1, j + 1] = new
         else:
             s4[s, i, j] = new
-        at = pl.ds(pl.multiple_of(((s * LON + i) * LAT + j) * ALT, ALT), ALT)
+        at = pl.ds(pl.multiple_of(s * CELLS, CELLS) + (i * LAT + j) * ALT, ALT)
         high, low = split(new)
         s_both[at, 0:HALF] = high
         s_both[at, HALF:WIDE] = low
 
     def cells(k, first, last, rows):
-        def one(n, c):
-            s = lax.div(n, last - first)
-            i = first + lax.rem(n, last - first)
-            for j in rows:
-                cell(k, s, i, j)
+        def one(s, c):
+            for i in range(first, last):
+                for j in rows:
+                    cell(k, s, i, j)
             return c
 
-        lax.fori_loop(0, 2 * (last - first), one, 0)
+        lax.fori_loop(0, 2, one, 0)
 
     def project(k):
         for s in range(2):
-            def part_of(b, c, s=s):
-                at = pl.ds(pl.multiple_of(b * 256, 256), 256)
-                both = s_both[pl.ds(pl.multiple_of(s * CELLS + b * 256, 256), 256)]
-                rays = slice(s * NEAR * RAYS, (s + 1) * NEAR * RAYS)
-                add = jnp.dot(h_high[rays, at], both, preferred_element_type=F32)
+            def part_of(t, c, s=s):
+                first = s * NEAR * RAYS + t * ROWS
+                rays = pl.ds(pl.multiple_of(first, ROWS), ROWS)
+                add = jnp.dot(h_high[rays], s_both[s * CELLS:(s + 1) * CELLS], preferred_element_type=F32)
                 add = add[:, 0:HALF] + add[:, HALF:WIDE]
-                add += jnp.dot(h_low[rays, at], both[:, 0:HALF], preferred_element_type=F32)
-                add = add.reshape(3, ROWS, HALF)
-
-                @pl.when(b == 0)
-                def _():
-                    near[k, s] = add
-
-                @pl.when(b > 0)
-                def _():
-                    near[k, s] += add
-
+                add += jnp.dot(
+                    h_low[rays], s_both[s * CELLS:(s + 1) * CELLS, 0:HALF], preferred_element_type=F32
+                )
+                near[k, s, t] = add
                 return c
 
-            lax.fori_loop(0, CELLS // 256, part_of, 0)
+            lax.fori_loop(0, 3, part_of, 0)
             out_both(ray_copy, k, s, begin)
 
     def turn(k):
@@ -325,7 +316,13 @@
         low = jnp.where(lane == 0, seen[k] - low, low) * scales[k]
         high = high * scales[k]
         rays = jnp.concatenate([low, high], axis=1)
-        gram[...] += jnp.dot(rays.T, rays, precision=highest, preferred_element_type=F32)
+        high, low = split(rays)
+        left_high, left_low = split(rays.T)
+        gram[...] += jnp.dot(
+            jnp.concatenate([left_high, left_high, left_low], axis=1),
+            jnp.concatenate([high, low, high], axis=0),
+            preferred_element_type=F32,
+        )
 
     swapped().wait_recv()
     send_edges(0, theirs)
@@ -377,6 +374,8 @@
 
     for d in range(1, n_lat):
         scatter(d).start()
+    for i in range(EARLY, BESIDE_SCATTER):
+        back(i).start()
     acc = packed[own(lat)]
     for d in range(1, n_lat):
         scatter(d).wait_recv()
@@ -384,15 +383,19 @@
     part[...] = acc
     for d in range(1, n_lon):
         across(d).start()
+    for i in range(BESIDE_SCATTER, BESIDE_ACROSS):
+        back(i).start()
     for d in range(1, n_lon):
         across(d).wait_recv()
         acc += got_lon[d]
     total[own(lat)] = acc
     for d in range(1, n_lat):
         gather(d).start()
+    for i in range(BESIDE_ACROSS, BESIDE_GATHER):
+        back(i).start()
     for d in range(1, n_lat):
         landed(d).wait_recv()
-    for i in range(EARLY, LON):
+    for i in range(BESIDE_GATHER, LON):
         back(i).start()
     u_high[...], u_low[...] = update_matrix(total, work, inverse, panel)
 
@@ -454,7 +457,7 @@
             pltpu.VMEM((STEPS, ROWS, HALF), F32),
             pltpu.VMEM((STEPS, ROWS, HALF), F32),
             pltpu.VMEM((2, 8, HALF), jnp.int32),
-            pltpu.VMEM((2, LON, HALF), F32),
+            pltpu.VMEM((2, 8, HALF), F32),
             pltpu.VMEM((WIDE, WIDE), F32),
             pltpu.VMEM((WIDE, WIDE), F32),
             pltpu.VMEM((PANEL, WIDE), F32),
@@ -621,7 +624,7 @@
     n_lon, n_lat = lax.axis_size("lon"), lax.axis_size("lat")
     forecast, u_high, u_low = window(
         n_lon, n_lat,
-        prior_state, courant, cell_survival_rate[None, :], geometry,
+        prior_state, courant.T, cell_survival_rate[None, :], geometry,
         entry_tile, entry_column, entry_segment, entry_counts, observed, obs_weight,
     )
     start_state, end_state = apply_update(

time: 134 us -> 122 us (0.910)
  Pallas kernels: 131 us -> 120 us
  local copies, waits for them, and re-layouts: 1.35 us -> 0 us
    pallas_call x1, Pallas kernels: 123 us -> 113 us  [window(): pl.pallas_call(functools.partial(window_kernel, n_lon, n_lat), out_shape=...]
    unnamed x1 -> x0, local copies, waits for them, and re-layouts: 1.35 us -> none
where the time goes in v6:
time: 122 us
  Pallas kernels  120 us (98%)
  between operations  1.45 us (1%)
    pallas_call x1, Pallas kernels, window(): pl.pallas_call(functools.partial(window_kernel, n_lon, n_lat), out_shape=...  113 us
    pallas_call x1, Pallas kernels, apply_update(): pl.pallas_call(apply_kernel, out_shape=(out, out), in_specs=[vmem, vmem,...  7.39 us

profile of v6, /device:TPU:1, one launch (start us, length us, event | category | flops | bytes accessed | tf_op | source)
XLA Modules:
  0.0 121.7 jit_solution(9992495452487349278)
XLA Ops:
  1.3 112.8 %window.1 = (f32[8,4,64,256]{3,2,1,0:T(8,128)}, bf16[256,256]{1,0:T(8,128)(2,1)}, bf16[256,256]{1,0:T(8,128)(2,1)}) custom-call(f32[8,4,64,256]{3,2,1,0:T(8,128)} %prior.1, f32[4,8]{1,0:T(4,128)} %bitcast.7, f32[1,64]{1,0:T(1,128)} %bitcast.8, f32[16,64,128]{2,1,0:T(8,128)} %geometry.1, s32[1,1,64]{2,1,0:T(1,128)} %entry_tile.1, s32[1,1,64]{2,1,0:T(1,128)} %entry_column.1, ...), custom_call_target="tpu_custom_call" | custom-call | flops 12000000000 | bytes 6000000 | tf_op jit(solution)/shard_map/window/pallas_call | solution.py:428
  114.1 7.4 %update.1 = (f32[2048,256]{1,0:T(8,128)}, f32[2048,256]{1,0:T(8,128)}) custom-call(bf16[256,256]{1,0:T(8,128)(2,1)} %get-tuple-element.7.u_high, bf16[256,256]{1,0:T(8,128)(2,1)} %get-tuple-element.8.u_low, f32[2048,256]{1,0:T(8,128)} %bitcast.6, f32[2048,256]{1,0:T(8,128)} %bitcast.11), custom_call_target="tpu_custom_call" | custom-call | flops 1700000000 | bytes 8400000 | tf_op jit(solution)/shard_map/update/pallas_call | solution.py:595

commit v7 on v6

--- a/solution.py
+++ b/solution.py
@@ -23,6 +23,7 @@
 PANEL = 16
 CELLS = LON * LAT * ALT
 CHUNKS = 4
+BUILD_FIRST = 7
 EARLY = 2
 BESIDE_SCATTER = 3
 BESIDE_ACROSS = 4
@@ -103,14 +104,14 @@
         pl.semaphore_signal(barrier, inc=1, device_id=at_lat(d), device_id_type=MESH)
     pl.semaphore_wait(barrier, n_lon + n_lat - 2)
 
-    def swap():
+    swaps = ((0, LON, 0, 1), (0, LON, LAT - 1, LAT), (LON - 1, LON, 1, LAT - 1), (0, LON - 1, 1, LAT - 1))
+
+    def swap(n, slot):
+        i, i_end, j, j_end = swaps[n]
         return remote(
-            prior.at[:, :, :, half(theirs)], s0.at[(mine,) + cells_of], swap_send, swap_recv, partner
-        )
-
-    def swapped():
-        return remote(
-            prior.at[:, :, :, half(theirs)], s0.at[(theirs,) + cells_of], swap_send, swap_recv, partner
+            prior.at[i:i_end, j:j_end, :, half(theirs)],
+            s0.at[slot, i + 1:i_end + 1, j + 1:j_end + 1],
+            swap_send.at[n], swap_recv.at[n], partner,
         )
 
     small = [
@@ -119,7 +120,8 @@
     ]
     for copy in small:
         copy.start()
-    swap().start()
+    for n in range(len(swaps)):
+        swap(n, mine).start()
 
     def back(i):
         return remote(
@@ -255,7 +257,11 @@
 
         return lax.fori_loop(0, PAIRS, build, c)
 
-    lax.fori_loop(0, 2 * NEAR, build_tile, 0)
+    lax.fori_loop(0, BUILD_FIRST, build_tile, 0)
+    for n in range(3):
+        swap(n, theirs).wait_recv()
+    send_edges(0, theirs)
+    lax.fori_loop(BUILD_FIRST, 2 * NEAR, build_tile, 0)
     gram[...] = jnp.zeros((WIDE, WIDE), F32)
 
     def cell(k, s, i, j):
@@ -284,8 +290,9 @@
         lax.fori_loop(0, 2, one, 0)
 
     def project(k):
-        for s in range(2):
-            def part_of(t, c, s=s):
+        for s, begin_at, step, number in ((0, 0, 2, 2), (1, 0, 2, 2), (0, 1, 0, 1), (1, 1, 0, 1)):
+            def part_of(n, c, s=s, begin_at=begin_at, step=step):
+                t = begin_at + step * n
                 first = s * NEAR * RAYS + t * ROWS
                 rays = pl.ds(pl.multiple_of(first, ROWS), ROWS)
                 add = jnp.dot(h_high[rays], s_both[s * CELLS:(s + 1) * CELLS], preferred_element_type=F32)
@@ -296,8 +303,9 @@
                 near[k, s, t] = add
                 return c
 
-            lax.fori_loop(0, 3, part_of, 0)
-            out_both(ray_copy, k, s, begin)
+            lax.fori_loop(0, number, part_of, 0)
+            if step:
+                out_both(ray_copy, k, s, begin)
 
     def turn(k):
         in_both(ray_landed, k, theirs)
@@ -324,8 +332,7 @@
             preferred_element_type=F32,
         )
 
-    swapped().wait_recv()
-    send_edges(0, theirs)
+    swap(3, theirs).wait_recv()
     for k in range(STEPS):
         cells(k, 1, LON, range(1, LAT - 1))
         for s in range(2):
@@ -345,11 +352,11 @@
         if k > 0:
             turn(k - 1)
         project(k)
-        if k > 1:
+        if 1 < k < STEPS - 1:
             add_gram(k - 2)
-    add_gram(STEPS - 2)
     turn(STEPS - 1)
-    add_gram(STEPS - 1)
+    for k in range(STEPS - 3, STEPS):
+        add_gram(k)
 
     packed[0:WIDE] = gram[:, 0:HALF]
     packed[WIDE:PACKED] = gram[HALF:WIDE, HALF:WIDE]
@@ -403,7 +410,8 @@
     for i in range(LON):
         back_landed(i).wait_recv()
         back(i).wait_send()
-    swap().wait_send()
+    for n in range(len(swaps)):
+        swap(n, mine).wait_send()
     for copy in small:
         copy.wait_send()
     for k in range(STEPS):
@@ -461,7 +469,7 @@
             pltpu.VMEM((WIDE, WIDE), F32),
             pltpu.VMEM((WIDE, WIDE), F32),
             pltpu.VMEM((PANEL, WIDE), F32),
-            dma, dma, dma, dma, dma((2,)), dma((2,)), dma((LON,)), dma((LON,)),
+            dma, dma, dma((4,)), dma((4,)), dma((2,)), dma((2,)), dma((LON,)), dma((LON,)),
             dma((STEPS, 2)), dma((STEPS, 2)),
             dma((STEPS, 2, 2)), dma((STEPS, 2, 2)),
             dma((STEPS, 2, 2)), dma((STEPS, 2, 2)),

time: 122 us -> 120 us (0.984)
  Pallas kernels: 120 us -> 118 us
    pallas_call x1, Pallas kernels: 113 us -> 111 us  [window(): pl.pallas_call(functools.partial(window_kernel, n_lon, n_lat), out_shape=...]
where the time goes in v7:
time: 120 us; the launch traced here: 119 us
  Pallas kernels  118 us (98%)
  between operations  1.45 us (1%)
    pallas_call x1, Pallas kernels, window(): pl.pallas_call(functools.partial(window_kernel, n_lon, n_lat), out_shape=...  111 us
    pallas_call x1, Pallas kernels, apply_update(): pl.pallas_call(apply_kernel, out_shape=(out, out), in_specs=[vmem, vmem,...  7.4 us

profile of v7, /device:TPU:1, one launch (start us, length us, event | category | flops | bytes accessed | tf_op | source)
XLA Modules:
  0.0 119.5 jit_solution(10427785765444147918)
XLA Ops:
  1.3 110.6 %window.1 = (f32[8,4,64,256]{3,2,1,0:T(8,128)}, bf16[256,256]{1,0:T(8,128)(2,1)}, bf16[256,256]{1,0:T(8,128)(2,1)}) custom-call(f32[8,4,64,256]{3,2,1,0:T(8,128)} %prior.1, f32[4,8]{1,0:T(4,128)} %bitcast.7, f32[1,64]{1,0:T(1,128)} %bitcast.8, f32[16,64,128]{2,1,0:T(8,128)} %geometry.1, s32[1,1,64]{2,1,0:T(1,128)} %entry_tile.1, s32[1,1,64]{2,1,0:T(1,128)} %entry_column.1, ...), custom_call_target="tpu_custom_call" | custom-call | flops 12000000000 | bytes 6000000 | tf_op jit(solution)/shard_map/window/pallas_call | solution.py:436
  111.9 7.4 %update.1 = (f32[2048,256]{1,0:T(8,128)}, f32[2048,256]{1,0:T(8,128)}) custom-call(bf16[256,256]{1,0:T(8,128)(2,1)} %get-tuple-element.7.u_high, bf16[256,256]{1,0:T(8,128)(2,1)} %get-tuple-element.8.u_low, f32[2048,256]{1,0:T(8,128)} %bitcast.6, f32[2048,256]{1,0:T(8,128)} %bitcast.11), custom_call_target="tpu_custom_call" | custom-call | flops 1700000000 | bytes 8400000 | tf_op jit(solution)/shard_map/update/pallas_call | solution.py:603

commit v8 on v7

--- a/solution.py
+++ b/solution.py
@@ -280,11 +280,14 @@
         s_both[at, 0:HALF] = high
         s_both[at, HALF:WIDE] = low
 
+    def one_slot(k, s, first, last, rows):
+        for i in range(first, last):
+            for j in rows:
+                cell(k, s, i, j)
+
     def cells(k, first, last, rows):
         def one(s, c):
-            for i in range(first, last):
-                for j in rows:
-                    cell(k, s, i, j)
+            one_slot(k, s, first, last, rows)
             return c
 
         lax.fori_loop(0, 2, one, 0)
@@ -332,9 +335,12 @@
             preferred_element_type=F32,
         )
 
+    one_slot(0, mine, 1, LON, range(1, LAT - 1))
     swap(3, theirs).wait_recv()
+    one_slot(0, theirs, 1, LON, range(1, LAT - 1))
     for k in range(STEPS):
-        cells(k, 1, LON, range(1, LAT - 1))
+        if k > 0:
+            cells(k, 1, LON, range(1, LAT - 1))
         for s in range(2):
             west_copy(k, s).wait_recv()
         cells(k, 0, 1, range(1, LAT - 1))

time: 120 us -> 119 us (level)
  no operation moved by 1% of the time
where the time goes in v8:
time: 119 us
  Pallas kernels  118 us (99%)
  between operations  1.45 us (1%)
    pallas_call x1, Pallas kernels, window(): pl.pallas_call(functools.partial(window_kernel, n_lon, n_lat), out_shape=...  110 us
    pallas_call x1, Pallas kernels, apply_update(): pl.pallas_call(apply_kernel, out_shape=(out, out), in_specs=[vmem, vmem,...  7.39 us

profile of v8, /device:TPU:1, one launch (start us, length us, event | category | flops | bytes accessed | tf_op | source)
XLA Modules:
  0.0 119.2 jit_solution(7552649256020414762)
XLA Ops:
  1.3 110.4 %window.1 = (f32[8,4,64,256]{3,2,1,0:T(8,128)}, bf16[256,256]{1,0:T(8,128)(2,1)}, bf16[256,256]{1,0:T(8,128)(2,1)}) custom-call(f32[8,4,64,256]{3,2,1,0:T(8,128)} %prior.1, f32[4,8]{1,0:T(4,128)} %bitcast.7, f32[1,64]{1,0:T(1,128)} %bitcast.8, f32[16,64,128]{2,1,0:T(8,128)} %geometry.1, s32[1,1,64]{2,1,0:T(1,128)} %entry_tile.1, s32[1,1,64]{2,1,0:T(1,128)} %entry_column.1, ...), custom_call_target="tpu_custom_call" | custom-call | flops 12000000000 | bytes 6000000 | tf_op jit(solution)/shard_map/window/pallas_call | solution.py:442
  111.7 7.4 %update.1 = (f32[2048,256]{1,0:T(8,128)}, f32[2048,256]{1,0:T(8,128)}) custom-call(bf16[256,256]{1,0:T(8,128)(2,1)} %get-tuple-element.7.u_high, bf16[256,256]{1,0:T(8,128)(2,1)} %get-tuple-element.8.u_low, f32[2048,256]{1,0:T(8,128)} %bitcast.6, f32[2048,256]{1,0:T(8,128)} %bitcast.11), custom_call_target="tpu_custom_call" | custom-call | flops 1700000000 | bytes 8400000 | tf_op jit(solution)/shard_map/update/pallas_call | solution.py:609
